TPU v7x, 32 devices: a whole 2x2x4 slice. The times are simulated.
32 devices in a mesh: dp: 8 (over z, y), fsdp: 4 (over x, core).
Axes of the slice: x: 2, y: 2, z: 4, core: 2. Of those that a mesh axis runs over, the one named last changes fastest.
Arguments:
- tokens: bfloat16 [32768, 512], P(('dp', 'fsdp')), may hold values from -6 to 6
- memory: bfloat16 [32768, 512], P(('dp', 'fsdp')), may hold values from -6 to 6
- token_seg: int32 [32, 1024], P(('dp', 'fsdp')), may hold values from 0 to 7, never falling along the last dimension, each value on 1 to 512 neighbouring positions
- token_pad: int32 [32, 1024], P(('dp', 'fsdp')), may hold values 0 or 1
- memory_seg: int32 [32, 1024], P(('dp', 'fsdp')), may hold values from 0 to 7, as said below
- memory_pad: int32 [32, 1024], P(('dp', 'fsdp')), may hold values from 0 to 1, as said below
- out_grad: bfloat16 [32768, 512], P(('dp', 'fsdp')), may hold values from -6 to 6
- self_q_w: bfloat16 [512, 512], P(('dp', 'fsdp')), may hold values from -0.25 to 0.25
- self_q_b: bfloat16 [512], P(('dp', 'fsdp')), may hold values from -1.75 to 1.75
- self_k_w: bfloat16 [512, 512], P(('dp', 'fsdp')), may hold values from -0.25 to 0.25
- self_v_w: bfloat16 [512, 512], P(('dp', 'fsdp')), may hold values from -0.25 to 0.25
- self_v_b: bfloat16 [512], P(('dp', 'fsdp')), may hold values from -1.75 to 1.75
- self_o_w: bfloat16 [512, 512], P(('dp', 'fsdp')), may hold values from -0.75 to 0.75
- self_o_b: bfloat16 [512], P(('dp', 'fsdp')), may hold values from -1.75 to 1.75
- norm1_gain: bfloat16 [512], P(('dp', 'fsdp')), may hold values from 0.25 to 1.75
- norm1_bias: bfloat16 [512], P(('dp', 'fsdp')), may hold values from -1.75 to 1.75
- cross_q_w: bfloat16 [512, 512], P(('dp', 'fsdp')), may hold values from -0.25 to 0.25
- cross_q_b: bfloat16 [512], P(('dp', 'fsdp')), may hold values from -1.75 to 1.75
- cross_k_w: bfloat16 [512, 512], P(('dp', 'fsdp')), may hold values from -0.25 to 0.25
- cross_v_w: bfloat16 [512, 512], P(('dp', 'fsdp')), may hold values from -0.25 to 0.25
- cross_v_b: bfloat16 [512], P(('dp', 'fsdp')), may hold values from -1.75 to 1.75
- cross_o_w: bfloat16 [512, 512], P(('dp', 'fsdp')), may hold values from -0.75 to 0.75
- cross_o_b: bfloat16 [512], P(('dp', 'fsdp')), may hold values from -1.75 to 1.75
- norm2_gain: bfloat16 [512], P(('dp', 'fsdp')), may hold values from 0.25 to 1.75
- norm2_bias: bfloat16 [512], P(('dp', 'fsdp')), may hold values from -1.75 to 1.75
- ffn_in_w: bfloat16 [512, 2048], P(('dp', 'fsdp')), may hold values from -0.25 to 0.25
- ffn_in_b: bfloat16 [2048], P(('dp', 'fsdp')), may hold values from -1.75 to 1.75
- ffn_out_w: bfloat16 [2048, 512], P(('dp', 'fsdp')), may hold values from -0.125 to 0.125
- ffn_out_b: bfloat16 [512], P(('dp', 'fsdp')), may hold values from -1.75 to 1.75
- norm3_gain: bfloat16 [512], P(('dp', 'fsdp')), may hold values from 0.25 to 1.75
- norm3_bias: bfloat16 [512], P(('dp', 'fsdp')), may hold values from -1.75 to 1.75
Outputs:
- layer_out: bfloat16 [32768, 512], P(('dp', 'fsdp'))
- tokens_grad: bfloat16 [32768, 512], P(('dp', 'fsdp'))
- memory_grad: bfloat16 [32768, 512], P(('dp', 'fsdp'))
- grad_self_q_w: float32 [512, 512], P(('dp', 'fsdp'))
- grad_self_q_b: float32 [512], P(('dp', 'fsdp'))
- grad_self_k_w: float32 [512, 512], P(('dp', 'fsdp'))
- grad_self_v_w: float32 [512, 512], P(('dp', 'fsdp'))
- grad_self_v_b: float32 [512], P(('dp', 'fsdp'))
- grad_self_o_w: float32 [512, 512], P(('dp', 'fsdp'))
- grad_self_o_b: float32 [512], P(('dp', 'fsdp'))
- grad_norm1_gain: float32 [512], P(('dp', 'fsdp'))
- grad_norm1_bias: float32 [512], P(('dp', 'fsdp'))
- grad_cross_q_w: float32 [512, 512], P(('dp', 'fsdp'))
- grad_cross_q_b: float32 [512], P(('dp', 'fsdp'))
- grad_cross_k_w: float32 [512, 512], P(('dp', 'fsdp'))
- grad_cross_v_w: float32 [512, 512], P(('dp', 'fsdp'))
- grad_cross_v_b: float32 [512], P(('dp', 'fsdp'))
- grad_cross_o_w: float32 [512, 512], P(('dp', 'fsdp'))
- grad_cross_o_b: float32 [512], P(('dp', 'fsdp'))
- grad_norm2_gain: float32 [512], P(('dp', 'fsdp'))
- grad_norm2_bias: float32 [512], P(('dp', 'fsdp'))
- grad_ffn_in_w: float32 [512, 2048], P(('dp', 'fsdp'))
- grad_ffn_in_b: float32 [2048], P(('dp', 'fsdp'))
- grad_ffn_out_w: float32 [2048, 512], P(('dp', 'fsdp'))
- grad_ffn_out_b: float32 [512], P(('dp', 'fsdp'))
- grad_norm3_gain: float32 [512], P(('dp', 'fsdp'))
- grad_norm3_bias: float32 [512], P(('dp', 'fsdp'))
Inputs may be any that keep to these rules, and one draw needn't show every extreme that they name: `memory_seg`: in each row the memory ids never fall and every id of 0 to 7 occurs. `memory_pad`: the first memory position of each document is never padding.
All inputs are finite; a program needn't handle non-finite values. No bound on the sum of `token_pad` on one device may be relied on, other than what follows from the above.
Results may differ from a plain program's by a relative error of at most 0.02.
Values may be sent and summed in bfloat16 or wider, within the bound.
A program may use at most 192 MiB of HBM per device.

v0:
```python
from functools import partial

import jax
import jax.numpy as jnp
from jax import lax
from jax.sharding import PartitionSpec as P

HEADS = 8


EPSILON = 1e-05
MASKED = -1e30


def layer_norm(values_in, gain_vec, shift_vec):
    center = values_in - jnp.mean(values_in, axis=-1, keepdims=True)
    spread = jnp.mean(center * center, axis=-1, keepdims=True)
    return center * lax.rsqrt(spread + EPSILON) * gain_vec + shift_vec


def linear(inputs, weight):
    return jnp.dot(inputs, weight, preferred_element_type=jnp.float32)


def linear_back(grad_rows, weight):
    return jnp.einsum("te,de->td", grad_rows, weight, preferred_element_type=jnp.float32)


def weight_grad(inputs, grad_rows):
    return jnp.einsum("td,te->de", inputs, grad_rows, preferred_element_type=jnp.float32)


def allowed_keys(query_seg, query_pos, key_seg, key_pad, causal):
    key_pos = jnp.arange(key_seg.shape[0])
    same_doc = query_seg[:, None] == key_seg[None, :]
    open_keys = key_pad[None, :] == 0
    if causal:
        return (
            same_doc
            & (key_pos[None, :] <= query_pos[:, None])
            & (open_keys | (key_pos[None, :] == query_pos[:, None]))
        )
    return same_doc & open_keys


def masked_scores(block_q, key_rows, allowed, score_scale):
    raw_scores = (
        jnp.einsum("qhd,khd->hqk", block_q, key_rows, preferred_element_type=jnp.float32)
        * score_scale
    )
    return jnp.where(allowed[None], raw_scores, MASKED)


def attend(query_rows, key_rows, value_rows, query_seg, key_seg, key_pad, causal):
    length = query_rows.shape[0]
    block_size = min(512, length)
    block_count = length // block_size
    score_scale = query_rows.shape[2] ** (-0.5)

    def per_block(pieces):
        block_q, block_seg, block_pos = pieces
        scores = masked_scores(
            block_q,
            key_rows,
            allowed_keys(block_seg, block_pos, key_seg, key_pad, causal),
            score_scale,
        )
        row_top = jnp.max(scores, axis=-1, keepdims=True)
        log_total = jnp.log(jnp.sum(jnp.exp(scores - row_top), axis=-1, keepdims=True)) + row_top
        prob_rows = jnp.exp(scores - log_total).astype(jnp.bfloat16)
        attended = jnp.einsum(
            "hqk,khd->qhd", prob_rows, value_rows, preferred_element_type=jnp.float32
        )
        return (attended.astype(jnp.bfloat16), log_total[..., 0])

    attended, log_totals = lax.map(
        per_block,
        (
            query_rows.reshape(block_count, block_size, query_rows.shape[1], query_rows.shape[2]),
            query_seg.reshape(block_count, block_size),
            jnp.arange(length).reshape(block_count, block_size),
        ),
    )
    return (attended.reshape(query_rows.shape), log_totals)


def attend_back(
    query_rows, key_rows, value_rows, grad_mixed, log_totals, query_seg, key_seg, key_pad, causal
):
    length = query_rows.shape[0]
    block_size = min(512, length)
    block_count = length // block_size
    score_scale = query_rows.shape[2] ** (-0.5)
    block_shape = (block_count, block_size, query_rows.shape[1], query_rows.shape[2])

    def per_block(carried, pieces):
        key_grad, value_grad = carried
        block_q, block_g, block_total, block_seg, block_pos = pieces
        scores = masked_scores(
            block_q,
            key_rows,
            allowed_keys(block_seg, block_pos, key_seg, key_pad, causal),
            score_scale,
        )
        prob_rows = jnp.exp(scores - block_total[..., None])
        value_grad = value_grad + jnp.einsum(
            "hqk,qhd->khd",
            prob_rows.astype(jnp.bfloat16),
            block_g,
            preferred_element_type=jnp.float32,
        )
        prob_grad = jnp.einsum(
            "qhd,khd->hqk", block_g, value_rows, preferred_element_type=jnp.float32
        )
        inner_sum = jnp.sum(prob_rows * prob_grad, axis=-1, keepdims=True)
        score_grad = (prob_rows * (prob_grad - inner_sum)).astype(jnp.bfloat16)
        query_grad = (
            jnp.einsum("hqk,khd->qhd", score_grad, key_rows, preferred_element_type=jnp.float32)
            * score_scale
        )
        key_grad = (
            key_grad
            + jnp.einsum("hqk,qhd->khd", score_grad, block_q, preferred_element_type=jnp.float32)
            * score_scale
        )
        return ((key_grad, value_grad), query_grad)

    zero_grad = jnp.zeros(key_rows.shape, jnp.float32)
    (key_grad, value_grad), query_grad = lax.scan(
        per_block,
        (zero_grad, zero_grad),
        (
            query_rows.reshape(block_shape),
            grad_mixed.reshape(block_shape),
            log_totals,
            query_seg.reshape(block_count, block_size),
            jnp.arange(length).reshape(block_count, block_size),
        ),
    )
    return (query_grad.reshape(query_rows.shape), key_grad, value_grad)


def split_heads(array_in, row_count):
    return array_in.reshape(
        row_count, array_in.shape[0] // row_count, HEADS, array_in.shape[1] // HEADS
    )


def sublayer_forward(weight_set, inputs, source, residual, query_seg, key_seg, key_pad, causal):
    query_w, query_b, key_w, value_w, value_b, output_w, output_b, norm_gain, norm_shift = (
        weight_set
    )
    row_count = query_seg.shape[0]
    query_rows = (linear(inputs, query_w) + query_b.astype(jnp.float32)).astype(jnp.bfloat16)
    key_rows = linear(source, key_w).astype(jnp.bfloat16)
    value_rows = (linear(source, value_w) + value_b.astype(jnp.float32)).astype(jnp.bfloat16)

    def per_row(pieces):
        return attend(pieces[0], pieces[1], pieces[2], pieces[3], pieces[4], pieces[5], causal)

    attended, log_totals = lax.map(
        per_row,
        (
            split_heads(query_rows, row_count),
            split_heads(key_rows, row_count),
            split_heads(value_rows, row_count),
            query_seg,
            key_seg,
            key_pad,
        ),
    )
    attended = attended.reshape(inputs.shape[0], -1)
    summed = residual + linear(attended, output_w) + output_b.astype(jnp.float32)
    normed = layer_norm(summed, norm_gain.astype(jnp.float32), norm_shift.astype(jnp.float32))
    return (normed, (query_rows, key_rows, value_rows, attended, log_totals, summed))


def sublayer_back(
    weight_set, kept_state, inputs, source, grad_normed, query_seg, key_seg, key_pad, causal
):
    query_w, query_b, key_w, value_w, value_b, output_w, output_b, norm_gain, norm_shift = (
        weight_set
    )
    query_rows, key_rows, value_rows, attended, log_totals, summed = kept_state
    row_count = query_seg.shape[0]
    _, pullback = jax.vjp(
        layer_norm, summed, norm_gain.astype(jnp.float32), norm_shift.astype(jnp.float32)
    )
    grad_summed, grad_gain, grad_shift = pullback(grad_normed)
    summed_low = grad_summed.astype(jnp.bfloat16)
    grad_output_w = weight_grad(attended, summed_low)
    grad_output_b = jnp.sum(grad_summed, axis=0)
    grad_mixed = linear_back(summed_low, output_w).astype(jnp.bfloat16)

    def per_row(pieces):
        return attend_back(
            pieces[0],
            pieces[1],
            pieces[2],
            pieces[3],
            pieces[4],
            pieces[5],
            pieces[6],
            pieces[7],
            causal,
        )

    grad_query, grad_keys, grad_values = lax.map(
        per_row,
        (
            split_heads(query_rows, row_count),
            split_heads(key_rows, row_count),
            split_heads(value_rows, row_count),
            split_heads(grad_mixed, row_count),
            log_totals,
            query_seg,
            key_seg,
            key_pad,
        ),
    )
    grad_query = grad_query.reshape(query_rows.shape).astype(jnp.bfloat16)
    grad_keys = grad_keys.reshape(key_rows.shape).astype(jnp.bfloat16)
    grad_values = grad_values.reshape(value_rows.shape).astype(jnp.bfloat16)
    grad_set = (
        weight_grad(inputs, grad_query),
        jnp.sum(grad_query.astype(jnp.float32), axis=0),
        weight_grad(source, grad_keys),
        weight_grad(source, grad_values),
        jnp.sum(grad_values.astype(jnp.float32), axis=0),
        grad_output_w,
        grad_output_b,
        grad_gain,
        grad_shift,
    )
    grad_inputs = grad_summed + linear_back(grad_query, query_w)
    grad_source = linear_back(grad_keys, key_w) + linear_back(grad_values, value_w)
    return (grad_set, grad_inputs, grad_source)


def ffn_forward(weight_set, inputs_low, residual):
    in_w, in_b, out_w, out_b, norm_gain, norm_shift = weight_set
    hidden = linear(inputs_low, in_w) + in_b.astype(jnp.float32)
    active = jax.nn.gelu(hidden, approximate=False).astype(jnp.bfloat16)
    summed = residual + linear(active, out_w) + out_b.astype(jnp.float32)
    normed = layer_norm(summed, norm_gain.astype(jnp.float32), norm_shift.astype(jnp.float32))
    return (normed, (hidden, active, summed))


def ffn_back(weight_set, kept_state, inputs_low, grad_normed):
    in_w, in_b, out_w, out_b, norm_gain, norm_shift = weight_set
    hidden, active, summed = kept_state
    _, pullback = jax.vjp(
        layer_norm, summed, norm_gain.astype(jnp.float32), norm_shift.astype(jnp.float32)
    )
    grad_summed, grad_gain, grad_shift = pullback(grad_normed)
    summed_low = grad_summed.astype(jnp.bfloat16)
    grad_active = linear_back(summed_low, out_w)
    _, gelu_pull = jax.vjp(partial(jax.nn.gelu, approximate=False), hidden)
    grad_hidden = gelu_pull(grad_active)[0].astype(jnp.bfloat16)
    grad_set = (
        weight_grad(inputs_low, grad_hidden),
        jnp.sum(grad_hidden.astype(jnp.float32), axis=0),
        weight_grad(active, summed_low),
        jnp.sum(grad_summed, axis=0),
        grad_gain,
        grad_shift,
    )
    grad_inputs = grad_summed + linear_back(grad_hidden, in_w)
    return (grad_set, grad_inputs)


def local(
    tokens,
    memory,
    token_seg,
    token_pad,
    memory_seg,
    memory_pad,
    out_grad,
    self_q_w,
    self_q_b,
    self_k_w,
    self_v_w,
    self_v_b,
    self_o_w,
    self_o_b,
    norm1_gain,
    norm1_bias,
    cross_q_w,
    cross_q_b,
    cross_k_w,
    cross_v_w,
    cross_v_b,
    cross_o_w,
    cross_o_b,
    norm2_gain,
    norm2_bias,
    ffn_in_w,
    ffn_in_b,
    ffn_out_w,
    ffn_out_b,
    norm3_gain,
    norm3_bias,
):
    self_set = (
        lax.all_gather(self_q_w, ("dp", "fsdp"), axis=0, tiled=True),
        lax.all_gather(self_q_b, ("dp", "fsdp"), axis=0, tiled=True),
        lax.all_gather(self_k_w, ("dp", "fsdp"), axis=0, tiled=True),
        lax.all_gather(self_v_w, ("dp", "fsdp"), axis=0, tiled=True),
        lax.all_gather(self_v_b, ("dp", "fsdp"), axis=0, tiled=True),
        lax.all_gather(self_o_w, ("dp", "fsdp"), axis=0, tiled=True),
        lax.all_gather(self_o_b, ("dp", "fsdp"), axis=0, tiled=True),
        lax.all_gather(norm1_gain, ("dp", "fsdp"), axis=0, tiled=True),
        lax.all_gather(norm1_bias, ("dp", "fsdp"), axis=0, tiled=True),
    )
    first_norm, self_state = sublayer_forward(
        self_set, tokens, tokens, tokens.astype(jnp.float32), token_seg, token_seg, token_pad, True
    )
    first_low = first_norm.astype(jnp.bfloat16)
    cross_set = (
        lax.all_gather(cross_q_w, ("dp", "fsdp"), axis=0, tiled=True),
        lax.all_gather(cross_q_b, ("dp", "fsdp"), axis=0, tiled=True),
        lax.all_gather(cross_k_w, ("dp", "fsdp"), axis=0, tiled=True),
        lax.all_gather(cross_v_w, ("dp", "fsdp"), axis=0, tiled=True),
        lax.all_gather(cross_v_b, ("dp", "fsdp"), axis=0, tiled=True),
        lax.all_gather(cross_o_w, ("dp", "fsdp"), axis=0, tiled=True),
        lax.all_gather(cross_o_b, ("dp", "fsdp"), axis=0, tiled=True),
        lax.all_gather(norm2_gain, ("dp", "fsdp"), axis=0, tiled=True),
        lax.all_gather(norm2_bias, ("dp", "fsdp"), axis=0, tiled=True),
    )
    second_norm, cross_state = sublayer_forward(
        cross_set, first_low, memory, first_norm, token_seg, memory_seg, memory_pad, False
    )
    second_low = second_norm.astype(jnp.bfloat16)
    ffn_set = (
        lax.all_gather(ffn_in_w, ("dp", "fsdp"), axis=0, tiled=True),
        lax.all_gather(ffn_in_b, ("dp", "fsdp"), axis=0, tiled=True),
        lax.all_gather(ffn_out_w, ("dp", "fsdp"), axis=0, tiled=True),
        lax.all_gather(ffn_out_b, ("dp", "fsdp"), axis=0, tiled=True),
        lax.all_gather(norm3_gain, ("dp", "fsdp"), axis=0, tiled=True),
        lax.all_gather(norm3_bias, ("dp", "fsdp"), axis=0, tiled=True),
    )
    layer_out, ffn_state = ffn_forward(ffn_set, second_low, second_norm)
    ffn_set = (
        lax.all_gather(ffn_in_w, ("dp", "fsdp"), axis=0, tiled=True),
        lax.all_gather(ffn_in_b, ("dp", "fsdp"), axis=0, tiled=True),
        lax.all_gather(ffn_out_w, ("dp", "fsdp"), axis=0, tiled=True),
        lax.all_gather(ffn_out_b, ("dp", "fsdp"), axis=0, tiled=True),
        lax.all_gather(norm3_gain, ("dp", "fsdp"), axis=0, tiled=True),
        lax.all_gather(norm3_bias, ("dp", "fsdp"), axis=0, tiled=True),
    )
    ffn_grad, grad_second = ffn_back(ffn_set, ffn_state, second_low, out_grad.astype(jnp.float32))
    ffn_shards = (
        lax.psum_scatter(ffn_grad[0], ("dp", "fsdp"), scatter_dimension=0, tiled=True),
        lax.psum_scatter(ffn_grad[1], ("dp", "fsdp"), scatter_dimension=0, tiled=True),
        lax.psum_scatter(ffn_grad[2], ("dp", "fsdp"), scatter_dimension=0, tiled=True),
        lax.psum_scatter(ffn_grad[3], ("dp", "fsdp"), scatter_dimension=0, tiled=True),
        lax.psum_scatter(ffn_grad[4], ("dp", "fsdp"), scatter_dimension=0, tiled=True),
        lax.psum_scatter(ffn_grad[5], ("dp", "fsdp"), scatter_dimension=0, tiled=True),
    )
    cross_set = (
        lax.all_gather(cross_q_w, ("dp", "fsdp"), axis=0, tiled=True),
        lax.all_gather(cross_q_b, ("dp", "fsdp"), axis=0, tiled=True),
        lax.all_gather(cross_k_w, ("dp", "fsdp"), axis=0, tiled=True),
        lax.all_gather(cross_v_w, ("dp", "fsdp"), axis=0, tiled=True),
        lax.all_gather(cross_v_b, ("dp", "fsdp"), axis=0, tiled=True),
        lax.all_gather(cross_o_w, ("dp", "fsdp"), axis=0, tiled=True),
        lax.all_gather(cross_o_b, ("dp", "fsdp"), axis=0, tiled=True),
        lax.all_gather(norm2_gain, ("dp", "fsdp"), axis=0, tiled=True),
        lax.all_gather(norm2_bias, ("dp", "fsdp"), axis=0, tiled=True),
    )
    cross_grad, grad_first, memory_grad = sublayer_back(
        cross_set,
        cross_state,
        first_low,
        memory,
        grad_second,
        token_seg,
        memory_seg,
        memory_pad,
        False,
    )
    cross_shards = (
        lax.psum_scatter(cross_grad[0], ("dp", "fsdp"), scatter_dimension=0, tiled=True),
        lax.psum_scatter(cross_grad[1], ("dp", "fsdp"), scatter_dimension=0, tiled=True),
        lax.psum_scatter(cross_grad[2], ("dp", "fsdp"), scatter_dimension=0, tiled=True),
        lax.psum_scatter(cross_grad[3], ("dp", "fsdp"), scatter_dimension=0, tiled=True),
        lax.psum_scatter(cross_grad[4], ("dp", "fsdp"), scatter_dimension=0, tiled=True),
        lax.psum_scatter(cross_grad[5], ("dp", "fsdp"), scatter_dimension=0, tiled=True),
        lax.psum_scatter(cross_grad[6], ("dp", "fsdp"), scatter_dimension=0, tiled=True),
        lax.psum_scatter(cross_grad[7], ("dp", "fsdp"), scatter_dimension=0, tiled=True),
        lax.psum_scatter(cross_grad[8], ("dp", "fsdp"), scatter_dimension=0, tiled=True),
    )
    self_set = (
        lax.all_gather(self_q_w, ("dp", "fsdp"), axis=0, tiled=True),
        lax.all_gather(self_q_b, ("dp", "fsdp"), axis=0, tiled=True),
        lax.all_gather(self_k_w, ("dp", "fsdp"), axis=0, tiled=True),
        lax.all_gather(self_v_w, ("dp", "fsdp"), axis=0, tiled=True),
        lax.all_gather(self_v_b, ("dp", "fsdp"), axis=0, tiled=True),
        lax.all_gather(self_o_w, ("dp", "fsdp"), axis=0, tiled=True),
        lax.all_gather(self_o_b, ("dp", "fsdp"), axis=0, tiled=True),
        lax.all_gather(norm1_gain, ("dp", "fsdp"), axis=0, tiled=True),
        lax.all_gather(norm1_bias, ("dp", "fsdp"), axis=0, tiled=True),
    )
    self_grad, grad_inputs, grad_source = sublayer_back(
        self_set, self_state, tokens, tokens, grad_first, token_seg, token_seg, token_pad, True
    )
    tokens_grad = grad_inputs + grad_source
    self_shards = (
        lax.psum_scatter(self_grad[0], ("dp", "fsdp"), scatter_dimension=0, tiled=True),
        lax.psum_scatter(self_grad[1], ("dp", "fsdp"), scatter_dimension=0, tiled=True),
        lax.psum_scatter(self_grad[2], ("dp", "fsdp"), scatter_dimension=0, tiled=True),
        lax.psum_scatter(self_grad[3], ("dp", "fsdp"), scatter_dimension=0, tiled=True),
        lax.psum_scatter(self_grad[4], ("dp", "fsdp"), scatter_dimension=0, tiled=True),
        lax.psum_scatter(self_grad[5], ("dp", "fsdp"), scatter_dimension=0, tiled=True),
        lax.psum_scatter(self_grad[6], ("dp", "fsdp"), scatter_dimension=0, tiled=True),
        lax.psum_scatter(self_grad[7], ("dp", "fsdp"), scatter_dimension=0, tiled=True),
        lax.psum_scatter(self_grad[8], ("dp", "fsdp"), scatter_dimension=0, tiled=True),
    )
    return (
        layer_out.astype(jnp.bfloat16),
        tokens_grad.astype(jnp.bfloat16),
        memory_grad.astype(jnp.bfloat16),
        self_shards[0],
        self_shards[1],
        self_shards[2],
        self_shards[3],
        self_shards[4],
        self_shards[5],
        self_shards[6],
        self_shards[7],
        self_shards[8],
        cross_shards[0],
        cross_shards[1],
        cross_shards[2],
        cross_shards[3],
        cross_shards[4],
        cross_shards[5],
        cross_shards[6],
        cross_shards[7],
        cross_shards[8],
        ffn_shards[0],
        ffn_shards[1],
        ffn_shards[2],
        ffn_shards[3],
        ffn_shards[4],
        ffn_shards[5],
    )


def solution(mesh):
    return jax.shard_map(
        local,
        mesh=mesh,
        in_specs=(
            P(("dp", "fsdp"), None),
            P(("dp", "fsdp"), None),
            P(("dp", "fsdp"), None),
            P(("dp", "fsdp"), None),
            P(("dp", "fsdp"), None),
            P(("dp", "fsdp"), None),
            P(("dp", "fsdp"), None),
            P(("dp", "fsdp"), None),
            P(("dp", "fsdp")),
            P(("dp", "fsdp"), None),
            P(("dp", "fsdp"), None),
            P(("dp", "fsdp")),
            P(("dp", "fsdp"), None),
            P(("dp", "fsdp")),
            P(("dp", "fsdp")),
            P(("dp", "fsdp")),
            P(("dp", "fsdp"), None),
            P(("dp", "fsdp")),
            P(("dp", "fsdp"), None),
            P(("dp", "fsdp"), None),
            P(("dp", "fsdp")),
            P(("dp", "fsdp"), None),
            P(("dp", "fsdp")),
            P(("dp", "fsdp")),
            P(("dp", "fsdp")),
            P(("dp", "fsdp"), None),
            P(("dp", "fsdp")),
            P(("dp", "fsdp"), None),
            P(("dp", "fsdp")),
            P(("dp", "fsdp")),
            P(("dp", "fsdp")),
        ),
        out_specs=(
            P(("dp", "fsdp"), None),
            P(("dp", "fsdp"), None),
            P(("dp", "fsdp"), None),
            P(("dp", "fsdp"), None),
            P(("dp", "fsdp")),
            P(("dp", "fsdp"), None),
            P(("dp", "fsdp"), None),
            P(("dp", "fsdp")),
            P(("dp", "fsdp"), None),
            P(("dp", "fsdp")),
            P(("dp", "fsdp")),
            P(("dp", "fsdp")),
            P(("dp", "fsdp"), None),
            P(("dp", "fsdp")),
            P(("dp", "fsdp"), None),
            P(("dp", "fsdp"), None),
            P(("dp", "fsdp")),
            P(("dp", "fsdp"), None),
            P(("dp", "fsdp")),
            P(("dp", "fsdp")),
            P(("dp", "fsdp")),
            P(("dp", "fsdp"), None),
            P(("dp", "fsdp")),
            P(("dp", "fsdp"), None),
            P(("dp", "fsdp")),
            P(("dp", "fsdp")),
            P(("dp", "fsdp")),
        ),
        check_vma=False,
    )
```

profile of v0, /device:TPU:0, one launch (start us, length us, event | category | flops | bytes accessed | tf_op | source)
XLA Modules:
  0.0 1895.7 jit_solution(11860527232559612494)
XLA Ops:
  21.2 42.7 %all-reduce.29 = (bf16[512]{0:T(512)(128)(2,1)S(1)}, bf16[512]{0:T(512)(128)(2,1)S(1)}, bf16[512]{0:T(512)(128)(2,1)S(1)}, bf16[512]{0:T(512)(128)(2,1)S(1)}, bf...) all-reduce(bf16[512]{0:T(512)(128)(2,1)S(1)} %dynamic-update-slice,, ...), channel_id=1, replica_groups=mesh['dp'=8,'fsdp'=4] {'dp','fsdp'}, use_global_device_ids=true, to_apply=%add | all-reduce | flops 8704 | bytes 34816
  63.9 42.7 %all_gather.85 = bf16[512,512]{1,0:T(8,128)(2,1)S(1)} all-gather(bf16[16,512]{1,0:T(8,128)(2,1)} %param.46), channel_id=1, replica_groups=mesh['dp'=8,'fsdp'=4] {'dp','fsdp'}, dimensions={0}, use_global_device_ids=true | all-gather | bytes 540672 | tf_op jit(solution)/shard_map/all_gather | solution.py:306
  115.8 40.9 %all_gather.88 = bf16[512,512]{1,0:T(8,128)(2,1)} all-gather(bf16[16,512]{1,0:T(8,128)(2,1)S(1)} %copy-done.90), channel_id=1, replica_groups=mesh['dp'=8,'fsdp'=4] {'dp','fsdp'}, dimensions={0}, use_global_device_ids=true | all-gather | bytes 540672 | tf_op jit(solution)/shard_map/all_gather | solution.py:309
  157.9 39.8 %all_gather.87 = bf16[512,512]{1,0:T(8,128)(2,1)S(1)} all-gather(bf16[16,512]{1,0:T(8,128)(2,1)S(1)} %copy-done.91), channel_id=1, replica_groups=mesh['dp'=8,'fsdp'=4] {'dp','fsdp'}, dimensions={0}, use_global_device_ids=true | all-gather | bytes 540672 | tf_op jit(solution)/shard_map/all_gather | solution.py:308
  202.4 31.7 %while.94 = (s32[]{:T(128)}, bf16[2,512,8,64]{1,3,2,0:T(8,128)(2,1)}, f32[2,8,512]{2,1,0:T(8,128)S(1)}, s32[2,512]{1,0:T(2,128)S(1)}, s32[1024]{0:T(1024)S(1)}, ...) while((s32[]{:T(128)}, ...), condition=%wide.region_3.4_spmd, body=%wide.region_0.3_spmd.sunk | while | flops 1123283968 | bytes 64117424 | solution.py:76
  204.0 4.1 fusion.202
  208.1 4.2 exponential_reduce_fusion.4
  212.4 4.9 fusion.203
  219.8 4.1 fusion.202
  223.9 4.2 exponential_reduce_fusion.4
  228.2 4.9 fusion.203
  237.5 38.1 %all_gather.90 = bf16[512,512]{1,0:T(8,128)(2,1)S(1)} all-gather(bf16[16,512]{1,0:T(8,128)(2,1)S(1)} %copy-done.92), channel_id=1, replica_groups=mesh['dp'=8,'fsdp'=4] {'dp','fsdp'}, dimensions={0}, use_global_device_ids=true | all-gather | bytes 540672 | tf_op jit(solution)/shard_map/all_gather | solution.py:311
  277.2 39.8 %all_gather.94 = bf16[512,512]{1,0:T(8,128)(2,1)S(1)} all-gather(bf16[16,512]{1,0:T(8,128)(2,1)S(1)} %copy-done.93), channel_id=1, replica_groups=mesh['dp'=8,'fsdp'=4] {'dp','fsdp'}, dimensions={0}, use_global_device_ids=true | all-gather | bytes 540672 | tf_op jit(solution)/shard_map/all_gather | solution.py:321
  320.6 3.9 reshape.664
  327.8 38.0 %all_gather.97 = bf16[512,512]{1,0:T(8,128)(2,1)S(1)} all-gather(bf16[16,512]{1,0:T(8,128)(2,1)S(1)} %copy-done.94), channel_id=1, replica_groups=mesh['dp'=8,'fsdp'=4] {'dp','fsdp'}, dimensions={0}, use_global_device_ids=true | all-gather | bytes 540672 | tf_op jit(solution)/shard_map/all_gather | solution.py:324
  365.8 39.4 %all_gather.96 = bf16[512,512]{1,0:T(8,128)(2,1)S(1)} all-gather(bf16[16,512]{1,0:T(8,128)(2,1)S(1)} %copy-done.95), channel_id=1, replica_groups=mesh['dp'=8,'fsdp'=4] {'dp','fsdp'}, dimensions={0}, use_global_device_ids=true | all-gather | bytes 540672 | tf_op jit(solution)/shard_map/all_gather | solution.py:323
  410.7 31.8 %while.95 = (s32[]{:T(128)}, bf16[2,512,8,64]{1,3,2,0:T(8,128)(2,1)}, f32[2,8,512]{2,1,0:T(8,128)S(1)}, s32[2,512]{1,0:T(2,128)S(1)}, s32[1024]{0:T(1024)S(1)}, ...) while((s32[]{:T(128)}, ...), condition=%wide.region_9.10_spmd, body=%wide.region_6.9_spmd.sunk | while | flops 1121186816 | bytes 64111272 | solution.py:76
  411.1 4.9 fusion.206
  416.0 4.2 exponential_reduce_fusion.5
  420.3 5.3 fusion.207
  427.0 4.9 fusion.206
  431.9 4.2 exponential_reduce_fusion.5
  436.2 5.3 fusion.207
  445.1 38.2 %all_gather.99 = bf16[512,512]{1,0:T(8,128)(2,1)S(1)} all-gather(bf16[16,512]{1,0:T(8,128)(2,1)S(1)} %copy-done.96), channel_id=1, replica_groups=mesh['dp'=8,'fsdp'=4] {'dp','fsdp'}, dimensions={0}, use_global_device_ids=true | all-gather | bytes 540672 | tf_op jit(solution)/shard_map/all_gather | solution.py:326
  487.1 24.5 %multiply_convert_fusion.2 = (bf16[1024,2048]{1,0:T(8,128)(2,1)}, f32[1024,2048]{1,0:T(8,128)}, f32[1024,2048]{1,0:T(8,128)}) fusion(f32[2048]{0:T(1024)S(1)} %convert_element_type.213, bf16[512,2048]{1,0:T(8,128)(2,1)} %all-gather.3.cloned.1.call-done, f32[1024,512]{0,1:T(8,128)} %copy-done.19, f32[512]{0:T(512)S(1)} %convert_element_type.211, ...), kind=kOutput, calls=%fused_computation.108 | convolution fusion | flops 2288517120 | bytes 25186304 | tf_op jit(solution)/shard_map/dot_general | solution.py:22
  511.6 6.0 fusion.96
  521.3 10.6 convert_reduce_fusion
  531.9 3.6 multiply_reduce_fusion.2
  548.0 93.8 %while.96 = (s32[]{:T(128)}, f32[1024,8,64]{0,2,1:T(8,128)}, f32[1024,8,64]{0,2,1:T(8,128)}, bf16[2,512,8,64]{1,3,2,0:T(8,128)(2,1)}, bf16[2,512,8,64]{1,3,2,0:T...) while((s32[]{:T(128)}, f32[1024,8,64]{0,2,1:T(8,128)}, ...), condition=%wide.region_20.21_spmd.clone, body=%wide.region_18.20_spmd.clone.sunk | while | flops 2726032384 | bytes 213223712 | solution.py:129
  548.6 3.8 fusion.217
  554.9 11.7 multiply_reduce_fusion.11
  566.7 9.4 multiply_convert_fusion.5
  576.0 6.7 bitcast_add_fusion.8
  582.7 8.0 fusion.218
  594.3 3.8 fusion.217
  600.7 11.8 multiply_reduce_fusion.11
  612.4 9.4 multiply_convert_fusion.5
  621.8 7.3 bitcast_add_fusion.8
  629.1 7.9 fusion.218
  637.0 4.6 bitcast_add_fusion.9
  663.4 94.2 %while.97 = (s32[]{:T(128)}, f32[1024,8,64]{0,2,1:T(8,128)}, f32[1024,8,64]{0,2,1:T(8,128)}, bf16[2,512,8,64]{1,3,2,0:T(8,128)(2,1)}, bf16[2,512,8,64]{1,3,2,0:T...) while((s32[]{:T(128)}, f32[1024,8,64]{0,2,1:T(8,128)}, ...), condition=%wide.region_25.26_spmd.clone, body=%wide.region_23.25_spmd.clone.sunk | while | flops 2728129536 | bytes 213099280 | solution.py:129
  666.0 3.8 fusion.228
  670.4 11.7 multiply_reduce_fusion.12
  682.1 9.4 multiply_convert_fusion.6
  691.5 6.7 bitcast_add_fusion.10
  698.2 7.6 fusion.230
  705.8 4.0 bitcast_add_fusion.11
  712.2 3.8 fusion.228
  716.6 11.8 multiply_reduce_fusion.12
  728.4 9.4 multiply_convert_fusion.6
  737.8 7.2 bitcast_add_fusion.10
  745.0 7.6 fusion.230
  752.6 4.8 bitcast_add_fusion.11
  788.9 6.6 fusion.80
  797.1 6.7 fusion.86
  809.7 38.1 %all-reduce.28 = (f32[512]{0:T(512)S(1)}, f32[512]{0:T(512)S(1)}, f32[512]{0:T(512)S(1)}, f32[512]{0:T(512)S(1)}, f32[512]{0:T(512)S(1)}, /*index=5*/f32[512]{0:...) all-reduce(f32[512]{0:T(512)S(1)} %reduce_sum.303, ...), channel_id=3, replica_groups=mesh['dp'=8,'fsdp'=4] {'dp','fsdp'}, use_global_device_ids=true, to_apply=%region_28.29.clone | all-reduce | flops 8704 | bytes 69632
  868.8 72.1 %reduce-scatter.23.cloned.1.call-done = f32[16,512]{1,0:T(8,128)} async-done(((f32[512,512]{1,0:T(8,128)}), f32[16,512]{1,0:T(8,128)}) %reduce-scatter.23.cloned.1.call-update) | async-done | bytes 32784 | tf_op jit(solution)/shard_map/reduce_scatter | solution.py:384
  940.9 133.5 %reduce-scatter.31.cloned.1.call-done = f32[16,512]{1,0:T(8,128)} async-done(((f32[512,512]{1,0:T(8,128)}), f32[16,512]{1,0:T(8,128)}) %reduce-scatter.31.cloned.1.call-update) | async-done | bytes 32784
  1074.4 133.6 %reduce-scatter.35.cloned.1.call-done = f32[16,512]{1,0:T(8,128)} async-done(((f32[512,512]{1,0:T(8,128)}), f32[16,512]{1,0:T(8,128)}) %reduce-scatter.35.cloned.1.call-update) | async-done | bytes 32784
  1208.0 133.7 %reduce-scatter.33.cloned.1.call-done = f32[16,512]{1,0:T(8,128)} async-done(((f32[512,512]{1,0:T(8,128)}), f32[16,512]{1,0:T(8,128)}) %reduce-scatter.33.cloned.1.call-update) | async-done | bytes 32784
  1341.7 133.6 %reduce-scatter.39.cloned.1.call-done = f32[16,512]{1,0:T(8,128)} async-done(((f32[512,512]{1,0:T(8,128)}), f32[16,512]{1,0:T(8,128)}) %reduce-scatter.39.cloned.1.call-update) | async-done | bytes 32784
  1475.2 133.5 %reduce-scatter.37.cloned.1.call-done = f32[16,512]{1,0:T(8,128)} async-done(((f32[512,512]{1,0:T(8,128)}), f32[16,512]{1,0:T(8,128)}) %reduce-scatter.37.cloned.1.call-update) | async-done | bytes 32784
  1608.7 139.8 %reduce-scatter.29.cloned.1.call-done = f32[64,512]{1,0:T(8,128)} async-done(((f32[2048,512]{1,0:T(8,128)}), f32[64,512]{1,0:T(8,128)}) %reduce-scatter.29.cloned.1.call-update) | async-done | bytes 131088 | tf_op jit(solution)/shard_map/reduce_scatter | solution.py:356
  1748.5 139.9 %reduce-scatter.27.cloned.1.call-done = f32[16,2048]{1,0:T(8,128)} async-done(((f32[512,2048]{1,0:T(8,128)}), f32[16,2048]{1,0:T(8,128)}) %reduce-scatter.27.cloned.1.call-update) | async-done | bytes 131088 | tf_op jit(solution)/shard_map/reduce_scatter | solution.py:354
  (474 shorter events, 172.2 us)
Async XLA Ops:
  7.2 398.8 %copy-start = (bf16[1024,512]{1,0:T(8,128)(2,1)S(1)}, bf16[1024,512]{1,0:T(8,128)(2,1)}, u32[]{:S(2)}) copy-start(bf16[1024,512]{1,0:T(8,128)(2,1)} %param.40) | copy-start | bytes 3145732
  7.2 101.9 %copy-start.51 = (bf16[1024,512]{1,0:T(8,128)(2,1)S(1)}, bf16[1024,512]{1,0:T(8,128)(2,1)}, u32[]{:S(2)}) copy-start(bf16[1024,512]{1,0:T(8,128)(2,1)} %param.39) | copy-start | bytes 3145732
  7.2 479.8 %all-gather.3.cloned.1.call-start = ((), (), s32[]{:S(2)}) async-start(), calls=%async_computation.10 | async-start | bytes 2162688 | tf_op jit(solution)/shard_map/all_gather | solution.py:336
  8.0 503.6 %all-gather.5.cloned.1.call-start = ((), (), s32[]{:S(2)}) async-start(), calls=%async_computation.11 | async-start | bytes 2162688 | tf_op jit(solution)/shard_map/all_gather | solution.py:338
  8.7 860.1 %reduce-scatter.25.cloned.1.call-start = ((), (), s32[]{:S(2)}) async-start(), calls=%async_computation.14 | async-start | bytes 1081344 | tf_op jit(solution)/shard_map/reduce_scatter | solution.py:389
  113.6 43.6 %copy-start.64 = (s32[1,1024]{1,0:T(1,128)S(1)}, s32[1,1024]{1,0:T(1,128)}, u32[]{:S(2)}) copy-start(s32[1,1024]{1,0:T(1,128)} %param.41) | copy-start | bytes 12292
  113.6 44.3 %copy-start.91 = (bf16[16,512]{1,0:T(8,128)(2,1)S(1)}, bf16[16,512]{1,0:T(8,128)(2,1)}, u32[]{:S(2)}) copy-start(bf16[16,512]{1,0:T(8,128)(2,1)} %param.48) | copy-start | bytes 49156
  157.9 42.6 %copy-start.42 = (bf16[512,512]{1,0:T(8,128)(2,1)S(1)}, bf16[512,512]{1,0:T(8,128)(2,1)}, u32[]{:S(2)}) copy-start(bf16[512,512]{1,0:T(8,128)(2,1)} %all_gather.88) | copy-start | bytes 1572868
  157.9 42.6 %copy-start.52 = (bf16[1024,512]{1,0:T(8,128)(2,1)S(1)}, bf16[1024,512]{1,0:T(8,128)(2,1)}, u32[]{:S(2)}) copy-start(bf16[1024,512]{1,0:T(8,128)(2,1)} %param.39) | copy-start | bytes 3145732
  208.1 4.3 copy-start.34
  223.9 4.3 copy-start.34
  234.1 3.4 copy-start.92
  234.1 41.5 %copy-start.61 = (bf16[1024,512]{0,1:T(8,128)(2,1)S(1)}, bf16[1024,512]{0,1:T(8,128)(2,1)}, u32[]{:S(2)}) copy-start(bf16[1024,512]{0,1:T(8,128)(2,1)} %copy.108) | copy-start | bytes 3145732
  237.5 38.9 %copy-start.56 = (bf16[64,8,2,512]{3,1,2,0:T(8,128)(2,1)}, bf16[64,8,2,512]{3,1,2,0:T(8,128)(2,1)S(1)}, u32[]{:S(2)}) copy-start(bf16[64,8,2,512]{3,1,2,0:T(8,128)(2,1)S(1)} %copy.161) | copy-start | bytes 3145732
  276.4 207.0 %copy-start.11 = (f32[1024,512]{0,1:T(8,128)}, f32[1024,512]{0,1:T(8,128)S(1)}, u32[]{:S(2)}) copy-start(f32[1024,512]{0,1:T(8,128)S(1)} %get-tuple-element.840) | copy-start | bytes 6291460
  276.5 206.9 %copy-start.74 = (f32[1024]{0:T(1024)}, f32[1024]{0:T(1024)S(1)}, u32[]{:S(2)}) copy-start(f32[1024]{0:T(1024)S(1)} %broadcast_multiply_fusion.2) | copy-start | bytes 12292
  276.8 43.8 %copy-start.82 = (f32[1024]{0:T(1024)}, f32[1024]{0:T(1024)S(1)}, u32[]{:S(2)}) copy-start(f32[1024]{0:T(1024)S(1)} %multiply_reduce_fusion.8) | copy-start | bytes 12292
  276.8 206.6 %copy-start.76 = (f32[1024]{0:T(1024)}, f32[1024]{0:T(1024)S(1)}, u32[]{:S(2)}) copy-start(f32[1024]{0:T(1024)S(1)} %fusion.83) | copy-start | bytes 12292
  276.8 206.6 %copy-start.86 = (f32[512]{0:T(512)}, f32[512]{0:T(512)S(1)}, u32[]{:S(2)}) copy-start(f32[512]{0:T(512)S(1)} %convert_element_type.201) | copy-start | bytes 6148
  324.4 41.4 %copy-start.95 = (bf16[16,512]{1,0:T(8,128)(2,1)S(1)}, bf16[16,512]{1,0:T(8,128)(2,1)}, u32[]{:S(2)}) copy-start(bf16[16,512]{1,0:T(8,128)(2,1)} %param.57) | copy-start | bytes 49156
  365.8 43.7 %copy-start.46 = (bf16[512,512]{1,0:T(8,128)(2,1)}, bf16[512,512]{1,0:T(8,128)(2,1)S(1)}, u32[]{:S(2)}) copy-start(bf16[512,512]{1,0:T(8,128)(2,1)S(1)} %all_gather.97) | copy-start | bytes 1572868
  416.0 4.3 copy-start.32
  431.9 4.3 copy-start.32
  445.1 39.3 %copy-start.59 = (bf16[64,8,2,512]{3,1,2,0:T(8,128)(2,1)}, bf16[64,8,2,512]{3,1,2,0:T(8,128)(2,1)S(1)}, u32[]{:S(2)}) copy-start(bf16[64,8,2,512]{3,1,2,0:T(8,128)(2,1)S(1)} %copy.162) | copy-start | bytes 3145732
  484.5 51.0 %copy-start.84 = (f32[1024]{0:T(1024)}, f32[1024]{0:T(1024)S(1)}, u32[]{:S(2)}) copy-start(f32[1024]{0:T(1024)S(1)} %broadcast_multiply_fusion.1) | copy-start | bytes 12292
  484.8 50.7 %copy-start.97 = (f32[1024]{0:T(1024)}, f32[1024]{0:T(1024)S(1)}, u32[]{:S(2)}) copy-start(f32[1024]{0:T(1024)S(1)} %fusion.84) | copy-start | bytes 12292
  485.1 50.4 %copy-start.99 = (f32[512]{0:T(512)}, f32[512]{0:T(512)S(1)}, u32[]{:S(2)}) copy-start(f32[512]{0:T(512)S(1)} %convert_element_type.210) | copy-start | bytes 6148
  485.2 26.4 %copy-start.109 = (f32[512]{0:T(512)}, f32[512]{0:T(512)S(1)}, u32[]{:S(2)}) copy-start(f32[512]{0:T(512)S(1)} %convert_element_type.211) | copy-start | bytes 6148
  521.3 10.6 copy-start.22
  521.3 10.6 copy-start.88
  521.3 10.6 copy-start.20
  521.3 10.6 copy-start.117
  531.9 3.7 copy-start.119
  541.4 327.4 %reduce-scatter.21.cloned.1.call-start = ((), (), s32[]{:S(2)}) async-start(), calls=%async_computation.12 | async-start | bytes 1081344 | tf_op jit(solution)/shard_map/reduce_scatter | solution.py:415
  576.0 14.6 copy-start.1
  582.7 8.0 copy-start.10
  621.8 15.2 copy-start.1
  629.1 7.9 copy-start.10
  637.0 4.6 copy-start.73
  644.5 3.4 copy-start.31
  644.6 3.4 copy-start.83
  644.6 3.4 copy-start.77
  651.0 289.9 %reduce-scatter.23.cloned.1.call-start = ((), (), s32[]{:S(2)}) async-start(), calls=%async_computation.13 | async-start | bytes 1081344 | tf_op jit(solution)/shard_map/reduce_scatter | solution.py:384
  658.9 4.5 copy-start.65
  658.9 4.5 copy-start.69
  662.3 412.1 %reduce-scatter.31.cloned.1.call-start = ((), (), s32[]{:S(2)}) async-start(), calls=%async_computation.17 | async-start | bytes 1081344
  666.0 3.8 copy-start.71
  691.5 6.7 copy-start.4
  691.5 14.3 copy-start.2
  712.2 3.8 copy-start.71
  737.8 7.3 copy-start.4
  737.8 14.8 copy-start.2
  757.6 3.6 copy-start.53
  765.7 442.3 %reduce-scatter.35.cloned.1.call-start = ((), (), s32[]{:S(2)}) async-start(), calls=%async_computation.19 | async-start | bytes 1081344
  771.6 570.1 %reduce-scatter.33.cloned.1.call-start = ((), (), s32[]{:S(2)}) async-start(), calls=%async_computation.18 | async-start | bytes 1081344
  777.6 697.7 %reduce-scatter.39.cloned.1.call-start = ((), (), s32[]{:S(2)}) async-start(), calls=%async_computation.21 | async-start | bytes 1081344
  783.2 825.5 %reduce-scatter.37.cloned.1.call-start = ((), (), s32[]{:S(2)}) async-start(), calls=%async_computation.20 | async-start | bytes 1081344
  788.8 959.7 %reduce-scatter.29.cloned.1.call-start = ((), (), s32[]{:S(2)}) async-start(), calls=%async_computation.16 | async-start | bytes 4325376 | tf_op jit(solution)/shard_map/reduce_scatter | solution.py:356
  795.5 1092.9 %reduce-scatter.27.cloned.1.call-start = ((), (), s32[]{:S(2)}) async-start(), calls=%async_computation.15 | async-start | bytes 4325376 | tf_op jit(solution)/shard_map/reduce_scatter | solution.py:354
  803.9 3.5 copy-start.81
  808.8 46.5 %copy-start.30 = (bf16[64,8,2,512]{3,1,2,0:T(8,128)(2,1)S(1)}, bf16[64,8,2,512]{3,1,2,0:T(8,128)(2,1)}, u32[]{:S(2)}) copy-start(bf16[64,8,2,512]{3,1,2,0:T(8,128)(2,1)} %copy-done.29) | copy-start | bytes 3145732
  809.6 47.5 %copy-start.26 = (bf16[1024,8,64]{0,2,1:T(8,128)(2,1)S(1)}, bf16[1024,8,64]{0,2,1:T(8,128)(2,1)}, u32[]{:S(2)}) copy-start(bf16[1024,8,64]{0,2,1:T(8,128)(2,1)} %copy-done.25) | copy-start | bytes 3145732
  847.7 9.4 copy-start.45
  860.9 4.3 copy-start.28
  (79 other events, 143.0 us)
Sparse Core Ops, SparseCore 0:
  10.9 59.3 all-gather.2
  73.2 55.9 all-gather.4
  541.5 132.2 reduce-scatter.24
  676.6 130.6 reduce-scatter.20
  810.0 130.8 reduce-scatter.22
  943.6 130.7 reduce-scatter.30
  1077.2 130.7 reduce-scatter.34
  1210.9 130.7 reduce-scatter.32
  1344.5 130.7 reduce-scatter.38
  1478.0 130.6 reduce-scatter.36
  1611.6 136.8 reduce-scatter.28
  1751.2 137.1 reduce-scatter.26
where the time goes:
time: 1900 us
  waiting for transfers between devices  1020 us (54%)
  blocking collectives  398 us (21%)
  matrix products  277 us (15%)
  local copies, waits for them, and re-layouts  108 us (6%)
  other arithmetic  74.3 us (4%)
    unnamed x17, waiting for transfers between devices  669 us
    reduce_scatter x1, waiting for transfers between devices, local(): lax.psum_scatter(ffn_grad[0], ('dp', 'fsdp'), scatter_dimension=0, tiled=...  140 us
    reduce_scatter x1, waiting for transfers between devices, local(): lax.psum_scatter(ffn_grad[2], ('dp', 'fsdp'), scatter_dimension=0, tiled=...  140 us
    unnamed x2, blocking collectives  80.7 us
    reduce_scatter x1, waiting for transfers between devices, local(): lax.psum_scatter(cross_grad[0], ('dp', 'fsdp'), scatter_dimension=0, tile...  72.1 us
    dot_general x8, matrix products, masked_scores(): jnp.einsum('qhd,khd->hqk', block_q, key_rows, preferred_element_type=jnp....  64.9 us
    unnamed x276, local copies, waits for them, and re-layouts  62.8 us
    all_gather x1, blocking collectives, local(): lax.all_gather(self_q_w, ('dp', 'fsdp'), axis=0, tiled=True)  42.7 us
  transfers between devices with their start and end apart: 12, of which 8 were waited for; matrix products, arithmetic and copies ran while one was open for 22% of the time, Pallas kernels for 0%

commit v1 on v0

v1 whole, which is shorter than its diff:
```python
from functools import partial

import jax
import jax.numpy as jnp
from jax import lax
from jax.experimental import pallas as pl
from jax.experimental.pallas import tpu as pltpu
from jax.sharding import PartitionSpec as P

HEADS = 8
EPSILON = 1e-05
MASKED = -1e30
AXES = ("dp", "fsdp")
MESH = pl.DeviceIdType.MESH
BF16 = jnp.bfloat16
F32 = jnp.float32
BLOCK = 256
VMEM_LIMIT = 58 << 20

(SELF_Q_B, SELF_V_B, SELF_O_B, NORM1_G, NORM1_B, CROSS_Q_B, CROSS_V_B, CROSS_O_B,
 NORM2_G, NORM2_B, FFN_OUT_B, NORM3_G, NORM3_B) = range(13)
FFN_IN_B = 15

BITS = ("zh", "zl", "y", "x", "c")
ORDERS = {
    "A": ("zh", "zl", "x", "y", "c"),
    "B": ("zh", "zl", "y", "x", "c"),
    "C": ("x", "zh", "zl", "y", "c"),
    "D": ("y", "zh", "zl", "x", "c"),
}
UNIT_ORDERS = "CDACDBCDACDBCDAB"
LAG = 4
UNITS = 16


def dot(left, right):
    return jnp.dot(left, right, preferred_element_type=F32)


def dot_nt(left, right):
    return lax.dot_general(left, right, (((1,), (1,)), ((), ())), preferred_element_type=F32)


def dot_tn(left, right):
    return lax.dot_general(left, right, (((0,), (0,)), ((), ())), preferred_element_type=F32)


def rows_at(index, size):
    return pl.ds(pl.multiple_of(index * size, size), size)


def loop(low, high, body):
    def step(index, carry):
        body(index)
        return carry

    lax.fori_loop(low, high, step, 0)


def whole(shape):
    return pl.BlockSpec(memory_space=pltpu.VMEM)


def any_space():
    return pl.BlockSpec(memory_space=pl.ANY)


def place():
    d = lax.axis_index("dp")
    f = lax.axis_index("fsdp")
    return d, f, {"zh": d // 4, "zl": (d // 2) % 2, "y": d % 2, "x": f // 2, "c": f % 2}


def flip(value, mask):
    return value + mask - 2 * mask * ((value // mask) % 2)


def partner(bit, d, f):
    return {
        "zh": (flip(d, 4), f),
        "zl": (flip(d, 2), f),
        "y": (flip(d, 1), f),
        "x": (d, flip(f, 2)),
        "c": (d, flip(f, 1)),
    }[bit]


def greet(d, f):
    barrier = pltpu.get_barrier_semaphore()
    for bit in BITS:
        pl.semaphore_signal(barrier, inc=1, device_id=partner(bit, d, f), device_id_type=MESH)
    pl.semaphore_wait(barrier, len(BITS))


def spread_vectors(packed, vec_ref, in_b_ref):
    flat = packed.reshape(512, 128)
    lane = lax.broadcasted_iota(jnp.int32, (128, 512), 0)
    column = lax.broadcasted_iota(jnp.int32, (128, 512), 1)
    pick = jnp.where((lane == column % 16) & (lane < 16), 1.0, 0.0).astype(BF16)
    spread = dot(flat, pick)
    row = lax.broadcasted_iota(jnp.int32, (512, 512), 0)
    col = lax.broadcasted_iota(jnp.int32, (512, 512), 1)
    kept = jnp.where(row // 16 == col // 16, spread, 0.0)
    vec_ref[...] = jnp.sum(kept.reshape(32, 16, 512), axis=0)
    device = lax.broadcasted_iota(jnp.int32, (32, 512), 0)
    source = lax.broadcasted_iota(jnp.int32, (32, 512), 1)
    choose = jnp.where(source == device * 16 + FFN_IN_B, 1.0, 0.0).astype(BF16)
    own = dot(choose, flat).astype(BF16)
    lane = lax.broadcasted_iota(jnp.int32, (128, 2048), 0)
    column = lax.broadcasted_iota(jnp.int32, (128, 2048), 1)
    pick = jnp.where((lane == column % 64) & (lane < 64), 1.0, 0.0).astype(BF16)
    spread = dot(own, pick)
    row = lax.broadcasted_iota(jnp.int32, (32, 2048), 0)
    col = lax.broadcasted_iota(jnp.int32, (32, 2048), 1)
    in_b_ref[...] = jnp.sum(jnp.where(row == col // 64, spread, 0.0), axis=0, keepdims=True)


def project(x_ref, weight, bias, out_ref, out_t_ref, scale=None):
    count = x_ref.shape[0] // BLOCK

    def body(i):
        rows = rows_at(i, BLOCK)
        value = dot(x_ref[rows, :], weight)
        if bias is not None:
            value = value + bias
        value = value.astype(BF16)
        if scale is not None:
            value = value * scale
        out_ref[rows, :] = value
        if out_t_ref is not None:
            out_t_ref[:, rows] = value.T

    loop(0, count, body)


PROJECTED = 9


def project_unit(unit, x_ref, m_ref, weight, vec_ref, outs):
    q, k, kt, v, vt, ck, ckt, cv, cvt = outs
    if unit == 0:
        project(x_ref, weight, vec_ref[SELF_Q_B : SELF_Q_B + 1, :], q, None, 0.125)
    if unit == 1:
        project(x_ref, weight, None, k, kt)
    if unit == 2:
        project(x_ref, weight, vec_ref[SELF_V_B : SELF_V_B + 1, :], v, vt)
    if unit == 5:
        project(m_ref, weight, None, ck, ckt)
    if unit == 6:
        project(m_ref, weight, vec_ref[CROSS_V_B : CROSS_V_B + 1, :], cv, cvt)


def gather_kernel(*refs):
    x_ref, m_ref, packed = refs[:3]
    shards = refs[3:13]
    o_s, o_c, o_i, o_o, vec_out, in_b_out = refs[13:19]
    outs = refs[19 : 19 + PROJECTED]
    rest = refs[19 + PROJECTED :]
    b_s, b_c, b_i, b_o, b_v = rest[:5]
    held = rest[5 : 5 + PROJECTED]
    send, recv, keep, done = rest[5 + PROJECTED :]
    d, f, me = place()
    own = tuple(me[bit] for bit in BITS)
    for i in range(4):
        b_s[own + (slice(None), slice(512 * i, 512 * i + 512))] = shards[i][...]
        b_c[own + (slice(None), slice(512 * i, 512 * i + 512))] = shards[4 + i][...]
    b_i[own] = shards[8][...]
    b_o[own] = shards[9][...]
    b_v[own] = packed[...]
    greet(d, f)

    buffers = [b_s] * 4 + [b_c] * 4 + [b_i] * 4 + [b_o] * 4 + [b_v]
    targets = [o_s] * 4 + [o_c] * 4 + [o_i] * 4 + [o_o] * 4

    def part(u, index):
        if u == UNITS:
            return index
        if buffers[u] is b_o:
            return index + (slice(16 * (u % 4), 16 * (u % 4) + 16), slice(None))
        return index + (slice(None), slice(512 * (u % 4), 512 * (u % 4) + 512))

    def copy(u, s):
        order = ORDERS["A" if u == UNITS else UNIT_ORDERS[u]]
        have = order[:s]
        index = part(u, tuple(slice(None) if bit in have else me[bit] for bit in BITS))
        return pltpu.make_async_remote_copy(
            src_ref=buffers[u].at[index],
            dst_ref=buffers[u].at[index],
            send_sem=send.at[u, s],
            recv_sem=recv.at[u, s],
            device_id=partner(order[s], d, f),
            device_id_type=MESH,
        )

    def put(u):
        index = part(u, (slice(None),) * 5)
        return pltpu.make_async_copy(buffers[u].at[index], targets[u].at[index], keep.at[u])

    def finished(u):
        if u == UNITS:
            spread_vectors(b_v[...].reshape(32, 16, 128), vec_out, in_b_out)
            return
        put(u).start()
        if u in (0, 1, 2, 5, 6):
            weight = buffers[u][part(u, (slice(None),) * 5)].reshape(512, 512)
            project_unit(u, x_ref, m_ref, weight, vec_out, held)

    steps = [(-2 + LAG * s, -s, UNITS, s) for s in range(6)]
    steps += [(u + LAG * s, -s, u, s) for u in range(UNITS) for s in range(6)]
    for _, _, u, s in sorted(steps):
        if s > 0:
            copy(u, s - 1).wait_recv()
        if s < 5:
            copy(u, s).start()
        else:
            finished(u)
    results = [
        pltpu.make_async_copy(held[i], outs[i], done.at[i]) for i in range(PROJECTED)
    ]
    for result in results:
        result.start()
    for u in range(UNITS + 1):
        for s in range(5):
            copy(u, s).wait_send()
        if u < UNITS:
            put(u).wait()
    for result in results:
        result.wait()


def gather(tokens, memory, packed, shards):
    rows, width = tokens.shape
    bits = (2,) * 5
    weights = [bits + (16, 2048)] * 3 + [bits + (64, 512)]
    straight, turned = (rows, width), (width, rows)
    projected = [straight, straight, turned, straight, turned, straight, turned, straight, turned]
    shapes = [jax.ShapeDtypeStruct(s, BF16) for s in weights]
    shapes += [jax.ShapeDtypeStruct((16, 512), F32), jax.ShapeDtypeStruct((1, 2048), F32)]
    shapes += [jax.ShapeDtypeStruct(s, BF16) for s in projected]
    result = pl.pallas_call(
        gather_kernel,
        out_shape=shapes,
        in_specs=[whole(None)] * 13,
        out_specs=[any_space()] * 4 + [whole(None)] * 2 + [any_space()] * PROJECTED,
        scratch_shapes=[pltpu.VMEM(s, BF16) for s in weights]
        + [pltpu.VMEM(bits + (16, 128), BF16)]
        + [pltpu.VMEM(s, BF16) for s in projected]
        + [
            pltpu.SemaphoreType.DMA((UNITS + 1, 5)),
            pltpu.SemaphoreType.DMA((UNITS + 1, 5)),
            pltpu.SemaphoreType.DMA((UNITS,)),
            pltpu.SemaphoreType.DMA((PROJECTED,)),
        ],
        compiler_params=pltpu.CompilerParams(
            collective_id=1, has_side_effects=True, vmem_limit_bytes=VMEM_LIMIT
        ),
        name="gather_project",
    )(tokens, memory, packed, *shards)
    w_s, w_c, w_i = (w.reshape(512, 2048) for w in result[:3])
    return w_s, w_c, w_i, result[3].reshape(2048, 512), result[4], result[5], result[6:]


def project_kernel(*refs):
    x_ref, m_ref, vec_ref, w_s, w_c = refs[:5]
    outs = refs[5:]
    for unit in (0, 1, 2, 5, 6):
        source = w_s if unit < 4 else w_c
        weight = source[:, 512 * (unit % 4) : 512 * (unit % 4) + 512]
        project_unit(unit, x_ref, m_ref, weight, vec_ref, outs)


def project_only(tokens, memory, vec, w_s, w_c):
    rows, width = tokens.shape
    straight, turned = (rows, width), (width, rows)
    projected = [straight, straight, turned, straight, turned, straight, turned, straight, turned]
    return pl.pallas_call(
        project_kernel,
        out_shape=[jax.ShapeDtypeStruct(s, BF16) for s in projected],
        in_specs=[whole(None)] * 5,
        out_specs=[whole(None)] * PROJECTED,
        compiler_params=pltpu.CompilerParams(vmem_limit_bytes=VMEM_LIMIT),
        name="project",
    )(tokens, memory, vec, w_s, w_c)


def lower_bound(seg_ref, value):
    last = seg_ref.shape[1] - 1

    def step(_, carry):
        low, high = carry
        middle = jnp.minimum((low + high) // 2, last)
        below = seg_ref[0, middle] < value
        return (jnp.where(below, middle + 1, low), jnp.where(below, high, middle))

    steps = (last + 1).bit_length()
    return lax.fori_loop(0, steps, step, (jnp.int32(0), jnp.int32(last + 1)))[0]


def key_blocks(query_seg, key_seg, block, causal):
    first = query_seg[0, block * BLOCK]
    low = lower_bound(key_seg, first) // BLOCK
    if causal:
        return low, block + 1
    last = query_seg[0, block * BLOCK + BLOCK - 1]
    high = (lower_bound(key_seg, last + 1) + BLOCK - 1) // BLOCK
    return low, high


def key_columns(seg_ref, pad_ref, column_ref):
    open_seg = jnp.where(pad_ref[...] == 0, seg_ref[...], -1).astype(F32)
    for i in range(seg_ref.shape[1] // 128):
        piece = jnp.broadcast_to(open_seg[:, 128 * i : 128 * i + 128], (128, 128)).T
        column_ref[128 * i : 128 * i + 128, :] = piece


def mask_block(bias_ref, column_ref, seg_ref, qb, kb, causal):
    query = seg_ref[:, rows_at(qb, BLOCK)].astype(F32)
    column = column_ref[rows_at(kb, BLOCK), :]
    allowed = jnp.concatenate([column] * (BLOCK // 128), axis=1) == query
    if causal:
        key_pos = kb * BLOCK + lax.broadcasted_iota(jnp.int32, (BLOCK, BLOCK), 0)
        query_pos = qb * BLOCK + lax.broadcasted_iota(jnp.int32, (BLOCK, BLOCK), 1)
        allowed = (allowed & (key_pos < query_pos)) | (key_pos == query_pos)
    bias_ref[...] = jnp.where(allowed, 0.0, MASKED)


def own_lanes(value, head):
    lane = lax.broadcasted_iota(jnp.int32, value.shape, 1)
    return jnp.where(lane // 64 == head, value, jnp.zeros_like(value))


def attend(q_ref, k_ref, vt_ref, seg_ref, column_ref, seg_s, key_seg_s, causal, out_ref, lse_ref,
           bias_ref, acc_ref, top_ref, sum_ref):
    def query_block(qb):
        rows = rows_at(qb, BLOCK)
        acc_ref[...] = jnp.zeros_like(acc_ref)
        top_ref[...] = jnp.full_like(top_ref, MASKED)
        sum_ref[...] = jnp.zeros_like(sum_ref)
        low, high = key_blocks(seg_s, key_seg_s, qb, causal)

        def key_block(kb):
            keys = rows_at(kb, BLOCK)
            mask_block(bias_ref, column_ref, seg_ref, qb, kb, causal)
            for slab in range(2):
                lanes = slice(256 * slab, 256 * slab + 256)
                key = k_ref[keys, lanes]
                query = q_ref[rows, lanes]
                for h in range(4):
                    head = 4 * slab + h
                    mine = slice(head, head + 1)
                    part = slice(64 * head, 64 * head + 64)
                    scores = dot_nt(key, own_lanes(query, h)) + bias_ref[...]
                    top = top_ref[mine, :]
                    new_top = jnp.maximum(top, jnp.max(scores, axis=0, keepdims=True))
                    prob = jnp.exp(scores - new_top)
                    fade = jnp.exp(top - new_top)
                    top_ref[mine, :] = new_top
                    sum_ref[mine, :] = sum_ref[mine, :] * fade + jnp.sum(prob, axis=0, keepdims=True)
                    acc_ref[part, :] = acc_ref[part, :] * fade + dot(vt_ref[part, keys], prob.astype(BF16))

        loop(low, high, key_block)
        total = sum_ref[...]
        lse_ref[:, rows] = top_ref[...] + jnp.log(total)
        scale = 1.0 / total
        for head in range(HEADS):
            part = slice(64 * head, 64 * head + 64)
            acc_ref[part, :] = acc_ref[part, :] * scale[head : head + 1, :]
        out_ref[rows, :] = acc_ref[...].astype(BF16).T

    loop(0, q_ref.shape[0] // BLOCK, query_block)


def attend_back(q_ref, k_ref, kt_ref, v_ref, g_ref, lse_ref, delta_ref, seg_ref, column_ref, seg_s,
                key_seg_s, causal, bias_ref, dqt_ref, dk_ref, dv_ref):
    dk_ref[...] = jnp.zeros_like(dk_ref)
    dv_ref[...] = jnp.zeros_like(dv_ref)
    dqt_ref[...] = jnp.zeros_like(dqt_ref)

    def query_block(qb):
        rows = rows_at(qb, BLOCK)
        low, high = key_blocks(seg_s, key_seg_s, qb, causal)

        def key_block(kb):
            keys = rows_at(kb, BLOCK)
            mask_block(bias_ref, column_ref, seg_ref, qb, kb, causal)
            for slab in range(2):
                lanes = slice(256 * slab, 256 * slab + 256)
                key = k_ref[keys, lanes]
                value = v_ref[keys, lanes]
                dk = dk_ref[keys, lanes]
                dv = dv_ref[keys, lanes]
                for h in range(4):
                    head = 4 * slab + h
                    mine = slice(head, head + 1)
                    part = slice(64 * head, 64 * head + 64)
                    query = own_lanes(q_ref[rows, lanes], h)
                    grad = own_lanes(g_ref[rows, lanes], h)
                    scores = dot_nt(key, query) + bias_ref[...]
                    prob = jnp.exp(scores - lse_ref[mine, rows])
                    prob_grad = dot_nt(value, grad)
                    score_grad = (prob * (prob_grad - delta_ref[mine, rows])).astype(BF16)
                    dv = dv + dot(prob.astype(BF16), grad)
                    dk = dk + dot(score_grad, query)
                    dqt_ref[part, rows] += dot(kt_ref[part, keys], score_grad)
                dk_ref[keys, lanes] = dk
                dv_ref[keys, lanes] = dv

        loop(low, high, key_block)

    loop(0, q_ref.shape[0] // BLOCK, query_block)


def normalize(summed):
    center = summed - jnp.mean(summed, axis=-1, keepdims=True)
    spread = jnp.mean(center * center, axis=-1, keepdims=True)
    inverse = lax.rsqrt(spread + EPSILON)
    return center * inverse, inverse


def normalize_back(grad, gain, normal, inverse):
    scaled = grad * gain
    mean = jnp.mean(scaled, axis=-1, keepdims=True)
    along = jnp.mean(scaled * normal, axis=-1, keepdims=True)
    return inverse * (scaled - mean - normal * along)


def column_sum(value):
    return jnp.sum(value, axis=0, keepdims=True)


def gelu_and_slope(hidden):
    size = jnp.abs(hidden) * (0.5 ** 0.5)
    t = 1.0 / (1.0 + 0.3275911 * size)
    bell = jnp.exp(-0.5 * hidden * hidden)
    poly = 1.061405429
    for c in (-1.453152027, 1.421413741, -0.284496736, 0.254829592):
        poly = poly * t + c
    tail = (0.5 * t) * poly * bell
    phi = jnp.where(hidden < 0.0, tail, 1.0 - tail)
    return hidden * phi, phi + hidden * (bell * 0.3989422804014327)


def row_delta(grad, mixed):
    head = lax.broadcasted_iota(jnp.int32, (16, 512), 0)
    lane = lax.broadcasted_iota(jnp.int32, (16, 512), 1)
    pick = jnp.where(lane // 64 == head, 1.0, 0.0).astype(BF16)
    product = grad.astype(F32) * mixed.astype(F32)
    high = product.astype(BF16)
    low = (product - high.astype(F32)).astype(BF16)
    return (dot_nt(pick, high) + dot_nt(pick, low))[:HEADS, :]


N_MIDDLE_IN = 29


def middle_kernel(*refs):
    (seg, pad, mseg, mpad, seg_s, mseg_s, vec, in_b, x_ref, q, k, vt) = refs[:12]
    late_in = refs[12:23]
    layer_out, first_low_out, grads_out, vec_grad, in_b_grad = refs[23:28]
    late_out = refs[28:36]
    scratch = refs[36:]
    late = scratch[:11]
    (kt, v, ck, ckt, cv, cvt, w_s, w_c, w_i, w_o, out_grad) = late
    (column, mcolumn, bias, acc, top, total, mixed, cmixed, lse, clse, delta, first_sum, first_norm,
     first_low, cq, second_low, d_second, d_low, active, slope, dqt, dv, low_a, grads,
     late_sem, out_sem) = scratch[11:]
    dk, low_b, low_c = first_norm, out_grad, d_low
    pieces = [buffer.at[:, 512 * i : 512 * i + 512] for buffer in (active, slope) for i in range(4)]
    dcq_o, dck_o, dcv_o, memory_grad, dq_o, dk_o, dv_o, tokens_grad = pieces
    copies = [pltpu.make_async_copy(late_in[i], late[i], late_sem.at[i]) for i in range(11)]
    for i in (6, 2, 5, 7, 8, 9, 10, 3, 4, 0, 1):
        copies[i].start()
    rows_total = x_ref.shape[0]
    blocks = rows_total // BLOCK

    def vector(index):
        return vec[index : index + 1, :]

    def add_vec(index, value):
        vec_grad[index : index + 1, :] += value

    vec_grad[...] = jnp.zeros_like(vec_grad)
    in_b_grad[...] = jnp.zeros_like(in_b_grad)
    key_columns(seg, pad, column)
    key_columns(mseg, mpad, mcolumn)

    attend(q, k, vt, seg, column, seg_s, seg_s, True, mixed, lse, bias, acc, top, total)
    copies[6].wait()
    copies[7].wait()

    def first(i):
        rows = rows_at(i, BLOCK)
        summed = x_ref[rows, :].astype(F32) + dot(mixed[rows, :], w_s[:, 1536:2048]) + vector(SELF_O_B)
        first_sum[rows, :] = summed
        normal, _ = normalize(summed)
        norm = normal * vector(NORM1_G) + vector(NORM1_B)
        first_norm[rows, :] = norm
        low = norm.astype(BF16)
        first_low[rows, :] = low
        query = (dot(low, w_c[:, 0:512]) + vector(CROSS_Q_B)).astype(BF16)
        cq[rows, :] = query * 0.125

    loop(0, blocks, first)
    first_low_copy = pltpu.make_async_copy(first_low, first_low_out, out_sem.at[0])
    first_low_copy.start()
    copies[2].wait()
    copies[5].wait()
    attend(cq, ck, cvt, seg, mcolumn, seg_s, mseg_s, False, cmixed, clse, bias, acc, top, total)
    copies[8].wait()
    copies[9].wait()
    copies[10].wait()

    def ffn(i):
        rows = rows_at(i, BLOCK)
        summed = first_norm[rows, :] + dot(cmixed[rows, :], w_c[:, 1536:2048]) + vector(CROSS_O_B)
        normal2, inverse2 = normalize(summed)
        second = normal2 * vector(NORM2_G) + vector(NORM2_B)
        low = second.astype(BF16)
        second_low[rows, :] = low
        third = second + vector(FFN_OUT_B)
        for c in range(4):
            cols = slice(512 * c, 512 * c + 512)
            hidden = dot(low, w_i[:, cols]) + in_b[:, cols]
            act, slant = gelu_and_slope(hidden)
            act = act.astype(BF16)
            active[rows, cols] = act
            slope[rows, cols] = slant.astype(BF16)
            third = third + dot(act, w_o[cols, :])
        normal3, inverse3 = normalize(third)
        layer_out[rows, :] = (normal3 * vector(NORM3_G) + vector(NORM3_B)).astype(BF16)
        grad = out_grad[rows, :].astype(F32)
        add_vec(NORM3_G, column_sum(grad * normal3))
        add_vec(NORM3_B, column_sum(grad))
        d_third = normalize_back(grad, vector(NORM3_G), normal3, inverse3)
        add_vec(FFN_OUT_B, column_sum(d_third))
        third_low = d_third.astype(BF16)
        d_low[rows, :] = third_low
        back = d_third
        for c in range(4):
            cols = slice(512 * c, 512 * c + 512)
            d_hidden = (dot_nt(third_low, w_o[cols, :]) * slope[rows, cols].astype(F32)).astype(BF16)
            slope[rows, cols] = d_hidden
            in_b_grad[:, cols] += column_sum(d_hidden.astype(F32))
            back = back + dot_nt(d_hidden, w_i[:, cols])
        add_vec(NORM2_G, column_sum(back * normal2))
        add_vec(NORM2_B, column_sum(back))
        d_sum = normalize_back(back, vector(NORM2_G), normal2, inverse2)
        add_vec(CROSS_O_B, column_sum(d_sum))
        d_second[rows, :] = d_sum
        sum_low = d_sum.astype(BF16)
        low_a[rows, :] = sum_low
        mix_grad = dot_nt(sum_low, w_c[:, 1536:2048]).astype(BF16)
        low_b[rows, :] = mix_grad
        delta[:, rows] = row_delta(mix_grad, cmixed[rows, :])

    loop(0, blocks, ffn)

    for c in range(4):
        cols = slice(512 * c, 512 * c + 512)
        grads[c] = dot_tn(second_low[...], slope[:, cols]).astype(BF16).reshape(32, 16, 512)
        value = dot_tn(active[:, cols], d_low[...]).astype(BF16).reshape(8, 4, 16, 512)
        for u in range(4):
            grads[4 + u, 8 * c : 8 * c + 8] = value[:, u]
    grads[8] = dot_tn(cmixed[...], low_a[...]).astype(BF16).reshape(32, 16, 512)
    grads_copy = pltpu.make_async_copy(grads.at[0:9], grads_out.at[0:9], out_sem.at[1])
    grads_copy.start()

    copies[3].wait()
    copies[4].wait()
    attend_back(cq, ck, ckt, cv, low_b, clse, delta, seg, mcolumn, seg_s, mseg_s, False, bias, dqt, dk, dv)

    def first_back(i):
        rows = rows_at(i, BLOCK)
        dq_low = (dqt[:, rows] * 0.125).astype(BF16).T
        dk_low = dk[rows, :].astype(BF16)
        dv_low = dv[rows, :].astype(BF16)
        dcq_o[rows, :] = dq_low
        dck_o[rows, :] = dk_low
        dcv_o[rows, :] = dv_low
        add_vec(CROSS_Q_B, column_sum(dq_low.astype(F32)))
        add_vec(CROSS_V_B, column_sum(dv_low.astype(F32)))
        memory_grad[rows, :] = (
            dot_nt(dk_low, w_c[:, 512:1024]) + dot_nt(dv_low, w_c[:, 1024:1536])
        ).astype(BF16)
        normal, inverse = normalize(first_sum[rows, :])
        back = d_second[rows, :] + dot_nt(dq_low, w_c[:, 0:512])
        add_vec(NORM1_G, column_sum(back * normal))
        add_vec(NORM1_B, column_sum(back))
        d_sum = normalize_back(back, vector(NORM1_G), normal, inverse)
        add_vec(SELF_O_B, column_sum(d_sum))
        d_second[rows, :] = d_sum
        sum_low = d_sum.astype(BF16)
        low_a[rows, :] = sum_low
        mix_grad = dot_nt(sum_low, w_s[:, 1536:2048]).astype(BF16)
        low_c[rows, :] = mix_grad
        delta[:, rows] = row_delta(mix_grad, mixed[rows, :])

    loop(0, blocks, first_back)
    results = [pltpu.make_async_copy(pieces[i], late_out[i], out_sem.at[3 + i]) for i in range(8)]
    for i in range(4):
        results[i].start()
    grads[9] = dot_tn(mixed[...], low_a[...]).astype(BF16).reshape(32, 16, 512)
    last_copy = pltpu.make_async_copy(grads.at[9:10], grads_out.at[9:10], out_sem.at[2])
    last_copy.start()

    copies[0].wait()
    copies[1].wait()
    attend_back(q, k, kt, v, low_c, lse, delta, seg, column, seg_s, seg_s, True, bias, dqt, dk, dv)

    def finish(i):
        rows = rows_at(i, BLOCK)
        dq_low = (dqt[:, rows] * 0.125).astype(BF16).T
        dk_low = dk[rows, :].astype(BF16)
        dv_low = dv[rows, :].astype(BF16)
        dq_o[rows, :] = dq_low
        dk_o[rows, :] = dk_low
        dv_o[rows, :] = dv_low
        add_vec(SELF_Q_B, column_sum(dq_low.astype(F32)))
        add_vec(SELF_V_B, column_sum(dv_low.astype(F32)))
        tokens_grad[rows, :] = (
            d_second[rows, :]
            + dot_nt(dq_low, w_s[:, 0:512])
            + dot_nt(dk_low, w_s[:, 512:1024])
            + dot_nt(dv_low, w_s[:, 1024:1536])
        ).astype(BF16)

    loop(0, blocks, finish)
    for i in range(4, 8):
        results[i].start()
    for i in range(8):
        results[i].wait()
    first_low_copy.wait()
    grads_copy.wait()
    last_copy.wait()


def middle(seg, pad, mseg, mpad, vec, in_b, tokens, projected, weights, out_grad):
    rows, width = tokens.shape
    q, k, kt, v, vt, ck, ckt, cv, cvt = projected
    wide, turned = (rows, width), (width, rows)
    smem = pl.BlockSpec(memory_space=pltpu.SMEM)
    late = [kt, v, ck, ckt, cv, cvt, *weights, out_grad]
    outs = [
        jax.ShapeDtypeStruct(wide, BF16),
        jax.ShapeDtypeStruct(wide, BF16),
        jax.ShapeDtypeStruct((10, 32, 16, 512), BF16),
        jax.ShapeDtypeStruct((16, 512), F32),
        jax.ShapeDtypeStruct((1, 2048), F32),
    ]
    outs += [jax.ShapeDtypeStruct(wide, BF16)] * 8
    big = lambda shape, kind: pltpu.VMEM(shape, kind)
    scratch = [big(a.shape, a.dtype) for a in late]
    scratch += [
        big((rows, 128), F32),
        big((rows, 128), F32),
        big((BLOCK, BLOCK), F32),
        big((width, BLOCK), F32),
        big((HEADS, BLOCK), F32),
        big((HEADS, BLOCK), F32),
        big(wide, BF16),
        big(wide, BF16),
        big((HEADS, rows), F32),
        big((HEADS, rows), F32),
        big((HEADS, rows), F32),
        big(wide, F32),
        big(wide, F32),
        big(wide, BF16),
        big(wide, BF16),
        big(wide, BF16),
        big(wide, F32),
        big(wide, BF16),
        big((rows, 2048), BF16),
        big((rows, 2048), BF16),
        big(turned, F32),
        big(wide, F32),
        big(wide, BF16),
        big((10, 32, 16, 512), BF16),
        pltpu.SemaphoreType.DMA((11,)),
        pltpu.SemaphoreType.DMA((11,)),
    ]
    return pl.pallas_call(
        middle_kernel,
        out_shape=outs,
        in_specs=[whole(None)] * 4 + [smem] * 2 + [whole(None)] * 6 + [any_space()] * 11,
        out_specs=[whole(None)] + [any_space()] * 2 + [whole(None)] * 2 + [any_space()] * 8,
        scratch_shapes=scratch,
        compiler_params=pltpu.CompilerParams(vmem_limit_bytes=VMEM_LIMIT),
        name="layer",
    )(seg, pad, mseg, mpad, seg, mseg, vec, in_b, tokens, q, k, vt, *late)


def pack_vectors(vec_grad, in_b_grad):
    row = lax.broadcasted_iota(jnp.int32, (32, 16, 512), 0)
    col = lax.broadcasted_iota(jnp.int32, (32, 16, 512), 2)
    own = jnp.where(row == col // 16, jnp.broadcast_to(vec_grad[None], (32, 16, 512)), 0.0)
    column = lax.broadcasted_iota(jnp.int32, (512, 128), 0)
    lane = lax.broadcasted_iota(jnp.int32, (512, 128), 1)
    pick = jnp.where((lane == column % 16) & (lane < 16), 1.0, 0.0).astype(BF16)
    packed = dot(own.reshape(512, 512).astype(BF16), pick)
    row = lax.broadcasted_iota(jnp.int32, (32, 2048), 0)
    col = lax.broadcasted_iota(jnp.int32, (32, 2048), 1)
    own = jnp.where(row == col // 64, jnp.broadcast_to(in_b_grad, (32, 2048)), 0.0).astype(BF16)
    column = lax.broadcasted_iota(jnp.int32, (2048, 128), 0)
    lane = lax.broadcasted_iota(jnp.int32, (2048, 128), 1)
    pick = jnp.where((lane == column % 64) & (lane < 64), 1.0, 0.0).astype(BF16)
    wide = dot(own, pick).astype(BF16)
    target = lax.broadcasted_iota(jnp.int32, (512, 32), 0)
    device = lax.broadcasted_iota(jnp.int32, (512, 32), 1)
    choose = jnp.where(target == device * 16 + FFN_IN_B, 1.0, 0.0).astype(BF16)
    return packed + dot(choose, wide)


def scatter_kernel(*refs):
    (x_ref, m_ref, f_ref, dcq, dck, dcv, dq, dk, dv, vec_grad, in_b_grad, ready) = refs[:12]
    sums, vec_sums = refs[12:14]
    (made, held, in0, in1, in2, in3, in4, g_v, v0, v1, v2, v3, v4, send, recv, keep) = refs[14:]
    d, f, me = place()
    greet(d, f)
    inbox = (in0, in1, in2, in3, in4)
    vec_inbox = (v0, v1, v2, v3, v4)
    n_ready = 10

    def order(u):
        return tuple(reversed(ORDERS["A" if u == UNITS else UNIT_ORDERS[u]]))

    def copy(u, s):
        bits = order(u)
        gone = bits[:s]
        if u == UNITS:
            index = tuple(me[b] if b in gone else 1 - me[b] if b == bits[s] else slice(None) for b in BITS)
            source, target = g_v.at[index], vec_inbox[s]
        elif s == 0:
            index = (slice(None),) * 4 + (1 - me["c"],)
            source = ready.at[(u,) + index] if u < n_ready else made.at[(u - n_ready,) + index]
            target = in0.at[u]
        else:
            index = tuple(me[b] if b in gone else 1 - me[b] if b == bits[s] else slice(None) for b in BITS[:4])
            source, target = held.at[(u,) + index], inbox[s].at[u]
        return pltpu.make_async_remote_copy(
            src_ref=source,
            dst_ref=target,
            send_sem=send.at[u, s],
            recv_sem=recv.at[u, s],
            device_id=partner(bits[s], d, f),
            device_id_type=MESH,
        )

    def own_half(u):
        index = (u,) + (slice(None),) * 4 + (me["c"],)
        return pltpu.make_async_copy(ready.at[index], held.at[u], keep.at[u])

    def add(u, s):
        bits = order(u)
        gone = bits[: s + 1]
        if u == UNITS:
            index = tuple(me[b] if b in gone else slice(None) for b in BITS)
            g_v[index] = g_v[index] + vec_inbox[s][...]
        elif s == 0:
            if u < n_ready:
                own_half(u).wait()
                mine = held[u]
            else:
                mine = made[(u - n_ready,) + (slice(None),) * 4 + (me["c"],)]
            held[u] = mine + in0[u]
        else:
            index = (u,) + tuple(me[b] if b in gone else slice(None) for b in BITS[:4])
            if s == 4:
                sums[u] = held[index].astype(F32) + in4[u].astype(F32)
            else:
                held[index] = held[index] + inbox[s][u]

    bits = (2,) * 5
    g_v[...] = pack_vectors(vec_grad[...], in_b_grad[...]).reshape(bits + (16, 128))

    def prepare(u):
        if u < n_ready:
            own_half(u).start()
        elif u < UNITS:
            left = (f_ref, m_ref, m_ref, x_ref, x_ref, x_ref)[u - n_ready]
            right = (dcq, dck, dcv, dq, dk, dv)[u - n_ready]
            made[u - n_ready] = dot_tn(left[...], right[...]).astype(BF16).reshape(bits + (16, 512))

    steps = [(u + LAG * s, -s, u, s) for u in range(UNITS + 1) for s in range(6)]
    for _, _, u, s in sorted(steps):
        if s == 0:
            prepare(u)
        if s > 0:
            copy(u, s - 1).wait_recv()
            add(u, s - 1)
        if s < 5:
            copy(u, s).start()
    for u in range(UNITS + 1):
        for s in range(5):
            copy(u, s).wait_send()
    vec_sums[...] = g_v[tuple(me[b] for b in BITS)]


def scatter(tokens, memory, first_low, back, vec_grad, in_b_grad, ready):
    bits = (2,) * 5
    unit = (16, 512)
    vec_unit = (16, 128)
    boxes = [(UNITS,) + (2,) * (4 - s) + unit for s in range(5)]
    return pl.pallas_call(
        scatter_kernel,
        out_shape=[
            jax.ShapeDtypeStruct((UNITS,) + unit, F32),
            jax.ShapeDtypeStruct(vec_unit, F32),
        ],
        in_specs=[whole(None)] * 11 + [any_space()],
        out_specs=[whole(None)] * 2,
        scratch_shapes=[pltpu.VMEM((6,) + bits + unit, BF16), pltpu.VMEM((UNITS,) + (2,) * 4 + unit, BF16)]
        + [pltpu.VMEM(b, BF16) for b in boxes]
        + [pltpu.VMEM(bits + vec_unit, F32)]
        + [pltpu.VMEM((2,) * (4 - s) + vec_unit, F32) for s in range(5)]
        + [
            pltpu.SemaphoreType.DMA((UNITS + 1, 5)),
            pltpu.SemaphoreType.DMA((UNITS + 1, 5)),
            pltpu.SemaphoreType.DMA((10,)),
        ],
        compiler_params=pltpu.CompilerParams(
            collective_id=2, has_side_effects=True, vmem_limit_bytes=VMEM_LIMIT
        ),
        name="grads_scatter",
    )(tokens, memory, first_low, *back, vec_grad, in_b_grad, ready.reshape((10,) + bits + unit))


def unpack_kernel(sums, vec_sums, *outs):
    matrices, vectors = outs[:10], outs[10:]
    for i, u in enumerate((13, 14, 15, 9, 10, 11, 12, 8)):
        matrices[i][...] = sums[u]
    for u in range(4):
        matrices[8][:, 512 * u : 512 * u + 512] = sums[u]
        matrices[9][16 * u : 16 * u + 16, :] = sums[4 + u]
    for i in range(13):
        vectors[i][...] = vec_sums[i : i + 1, 0:16]
    vectors[13][...] = vec_sums[FFN_IN_B : FFN_IN_B + 1, 0:64]


def unpack(sums, vec_sums):
    shapes = [(16, 512)] * 8 + [(16, 2048), (64, 512)] + [(1, 16)] * 13 + [(1, 64)]
    return pl.pallas_call(
        unpack_kernel,
        out_shape=[jax.ShapeDtypeStruct(s, F32) for s in shapes],
        in_specs=[whole(None)] * 2,
        out_specs=[whole(None)] * len(shapes),
        name="unpack",
    )(sums, vec_sums)


def weight_kernel(x_ref, m_ref, f_ref, dcq, dck, dcv, dq, dk, dv, out_ref):
    pairs = ((f_ref, dcq), (m_ref, dck), (m_ref, dcv), (x_ref, dq), (x_ref, dk), (x_ref, dv))
    for i, (left, right) in enumerate(pairs):
        out_ref[i] = dot_tn(left[...], right[...])


def local(
    tokens, memory, token_seg, token_pad, memory_seg, memory_pad, out_grad,
    self_q_w, self_q_b, self_k_w, self_v_w, self_v_b, self_o_w, self_o_b, norm1_gain, norm1_bias,
    cross_q_w, cross_q_b, cross_k_w, cross_v_w, cross_v_b, cross_o_w, cross_o_b, norm2_gain, norm2_bias,
    ffn_in_w, ffn_in_b, ffn_out_w, ffn_out_b, norm3_gain, norm3_bias, *, ring,
):
    vectors = (self_q_b, self_v_b, self_o_b, norm1_gain, norm1_bias, cross_q_b, cross_v_b, cross_o_b,
               norm2_gain, norm2_bias, ffn_out_b, norm3_gain, norm3_bias)
    shards = (self_q_w, self_k_w, self_v_w, self_o_w, cross_q_w, cross_k_w, cross_v_w, cross_o_w,
              ffn_in_w, ffn_out_w)
    if ring:
        packed = jnp.concatenate(
            [
                jnp.pad(jnp.stack(vectors), ((0, 2), (0, 112))),
                jnp.pad(ffn_in_b.reshape(1, 64), ((0, 0), (0, 64))),
            ]
        )
        w_s, w_c, w_i, w_o, vec, in_b, projected = gather(tokens, memory, packed, shards)
    else:
        get = partial(lax.all_gather, axis_name=AXES, axis=0, tiled=True)
        full = [get(w) for w in shards]
        w_s, w_c = jnp.concatenate(full[:4], 1), jnp.concatenate(full[4:8], 1)
        w_i, w_o = full[8:]
        vec = jnp.pad(jnp.stack([get(b) for b in vectors]).astype(F32), ((0, 3), (0, 0)))
        in_b = get(ffn_in_b).astype(F32).reshape(1, -1)
        projected = project_only(tokens, memory, vec, w_s, w_c)
    (layer_out, first_low, ready, vec_grad, in_b_grad, dcq, dck, dcv, memory_grad, dq, dk, dv,
     tokens_grad) = middle(
        token_seg, token_pad, memory_seg, memory_pad, vec, in_b, tokens, projected, (w_s, w_c, w_i, w_o), out_grad
    )
    back = (dcq, dck, dcv, dq, dk, dv)
    if ring:
        sums, vec_sums = scatter(tokens, memory, first_low, back, vec_grad, in_b_grad, ready)
        shards = unpack(sums, vec_sums)
        mats, vecs = shards[:10], [s.reshape(-1) for s in shards[10:]]
    else:
        give = partial(lax.psum_scatter, axis_name=AXES, scatter_dimension=0, tiled=True)
        made = pl.pallas_call(
            weight_kernel,
            out_shape=jax.ShapeDtypeStruct((6, 512, 512), F32),
            in_specs=[whole(None)] * 9,
            out_specs=whole(None),
            compiler_params=pltpu.CompilerParams(vmem_limit_bytes=VMEM_LIMIT),
            name="weight_grads",
        )(tokens, memory, first_low, *back)
        done = ready.astype(F32).reshape(10, 512, 512)
        in_w = done[:4].transpose(1, 0, 2).reshape(512, 2048)
        out_w = done[4:8].reshape(4, 32, 16, 512).transpose(1, 0, 2, 3).reshape(2048, 512)
        full = [made[3], made[4], made[5], done[9], made[0], made[1], made[2], done[8], in_w, out_w]
        mats = [give(g) for g in full]
        vecs = [give(vec_grad[i]) for i in range(13)] + [give(in_b_grad[0])]
    (g_sqw, g_skw, g_svw, g_sow, g_cqw, g_ckw, g_cvw, g_cow, g_iw, g_ow) = mats
    (g_sqb, g_svb, g_sob, g_n1g, g_n1b, g_cqb, g_cvb, g_cob, g_n2g, g_n2b, g_ob, g_n3g, g_n3b, g_ib) = vecs
    return (
        layer_out, tokens_grad, memory_grad,
        g_sqw, g_sqb, g_skw, g_svw, g_svb, g_sow, g_sob, g_n1g, g_n1b,
        g_cqw, g_cqb, g_ckw, g_cvw, g_cvb, g_cow, g_cob, g_n2g, g_n2b,
        g_iw, g_ib, g_ow, g_ob, g_n3g, g_n3b,
    )


def solution(mesh):
    ring = mesh.shape["dp"] == 8 and mesh.shape["fsdp"] == 4
    matrix, vector = P(AXES, None), P(AXES)
    return jax.shard_map(
        partial(local, ring=ring),
        mesh=mesh,
        in_specs=(
            (matrix,) * 7
            + (matrix, vector, matrix, matrix, vector, matrix, vector, vector, vector) * 2
            + (matrix, vector, matrix, vector, vector, vector)
        ),
        out_specs=(
            (matrix,) * 3
            + (matrix, vector, matrix, matrix, vector, matrix, vector, vector, vector) * 2
            + (matrix, vector, matrix, vector, vector, vector)
        ),
        check_vma=False,
    )
```

time: 1900 us -> 248 us (0.13)
  waiting for transfers between devices: 1020 us -> 0 us
  blocking collectives: 398 us -> 0 us
  matrix products: 277 us -> 0 us
  Pallas kernels: 0 us -> 246 us
  local copies, waits for them, and re-layouts: 108 us -> 1.54 us
  other arithmetic: 74.3 us -> 1.26 us
    unnamed x17 -> x0, waiting for transfers between devices: 669 us -> none
    reduce_scatter x5 -> x0, waiting for transfers between devices: 352 us -> none  [the longest x1 140 us: local(): lax.psum_scatter(ffn_grad[0], ('dp', 'fsdp'), scatter_dimension=0, tiled=...]
    all_gather x8 -> x0, blocking collectives: 317 us -> none  [the longest x1 42.7 us: local(): lax.all_gather(self_q_w, ('dp', 'fsdp'), axis=0, tiled=True)]
    dot_general x58 -> x0, matrix products: 277 us -> none  [the longest x8 64.9 us: masked_scores(): jnp.einsum('qhd,khd->hqk', block_q, key_rows, preferred_element_type=jnp....]
    pallas_call x0 -> x4, Pallas kernels: none -> 246 us  [the longest x1 121 us: middle(): pl.pallas_call(middle_kernel, out_shape=outs, in_specs=[whole(None)] * 4...]
    unnamed x2 -> x0, blocking collectives: 80.7 us -> none
    unnamed x276 -> x0, local copies, waits for them, and re-layouts: 62.8 us -> none
    convert_element_type x21 -> x0, other arithmetic: 38.2 us -> none  [the longest x4 37.5 us: per_block(): score_grad = (prob_rows * (prob_grad - inner_sum)).astype(jnp.bfloat16)]
  transfers between devices with their start and end apart: 12 -> 0, of which waited for: 8 -> 0; matrix products, arithmetic and copies ran while one was open for 22% -> 0% of each run, Pallas kernels for 0% -> 0%
where the time goes in v1:
time: 248 us; the launch traced here: 250 us
  Pallas kernels  246 us (99%)
    pallas_call x1, Pallas kernels, middle(): pl.pallas_call(middle_kernel, out_shape=outs, in_specs=[whole(None)] * 4...  121 us
    pallas_call x1, Pallas kernels, scatter(): pl.pallas_call(scatter_kernel, out_shape=[jax.ShapeDtypeStruct((UNITS,) +...  67 us
    pallas_call x1, Pallas kernels, gather(): pl.pallas_call(gather_kernel, out_shape=shapes, in_specs=[whole(None)] *...  57 us

profile of v1, /device:TPU:0, one launch (start us, length us, event | category | flops | bytes accessed | tf_op | source)
XLA Modules:
  0.0 250.1 jit_solution(11341907203237521514)
XLA Ops:
  0.7 1.5 stack.55
  2.2 1.3 fusion.2.refs_2_
  3.5 57.0 %gather_project.1 = (bf16[2,2,2,2,2,16,2048]{6,5,4,3,2,1,0:T(8,128)(2,1)}, bf16[2,2,2,2,2,16,2048]{6,5,4,3,2,1,0:T(8,128)(2,1)}, bf16[2,2,2,2,2,16,2048]{6,5,4,3...) custom-call(bf16[1024,512]{1,0:T(8,128)(2,1)} %refs_0_.5, ...), custom_call_target="tpu_custom_call" | custom-call | tf_op jit(solution)/shard_map/gather_project/pallas_call | solution.py:240
  60.4 120.6 %layer.1 = (bf16[1024,512]{1,0:T(8,128)(2,1)}, bf16[1024,512]{1,0:T(8,128)(2,1)}, bf16[10,32,16,512]{3,2,1,0:T(8,128)(2,1)}, f32[16,512]{1,0:T(8,128)}, f32[1,20...) custom-call(s32[1,1024]{1,0:T(1,128)} %refs_4_.3, ...), custom_call_target="tpu_custom_call" | custom-call | tf_op jit(solution)/shard_map/layer/pallas_call | solution.py:681
  181.0 67.0 %grads_scatter.1 = (f32[16,16,512]{2,1,0:T(8,128)}, f32[16,128]{1,0:T(8,128)}) custom-call(bf16[1024,512]{1,0:T(8,128)(2,1)} %refs_0_.5, bf16[1024,512]{1,0:T(8,128)(2,1)} %refs_1_.5, bf16[1024,512]{1,0:T(8,128)(2,1)} %get-tuple-element.99.refs_2_, bf16[1024,512]{1,0:T(8,128)(2,1)} %get-tuple-element.100.refs_3_, ...), custom_call_target="tpu_custom_call" | custom-call | tf_op jit(solution)/shard_map/grads_scatter/pallas_call | solution.py:803
  248.1 1.9 unpack.1
